TPU v7x, 512 devices: a whole 4x8x8 slice. The times are simulated.
512 devices in a mesh: prompt: 4 (over x), sample: 32 (over z, y_lo, core), head: 4 (over y_hi).
Axes of the slice: x: 4, y: 8 (y_hi: 4, y_lo: 2; y = y_hi * 2 + y_lo), z: 8, core: 2. Of those that a mesh axis runs over, the one named last changes fastest.
Arguments:
- comp_q: bfloat16 [4, 32, 128, 4096], P('prompt', 'sample', None, 'head'), may hold values from -6 to 6
- comp_k: bfloat16 [4, 32, 128, 512], P('prompt', 'sample', None, 'head'), may hold values from -6 to 6
- comp_v: bfloat16 [4, 32, 128, 512], P('prompt', 'sample', None, 'head'), may hold values from -6 to 6
- prompt_k: bfloat16 [4, 3072, 512], P('prompt', 'sample', 'head'), may hold values from -6 to 6
- prompt_v: bfloat16 [4, 3072, 512], P('prompt', 'sample', 'head'), may hold values from -6 to 6
- lengths: int32 [4, 32], P('prompt', 'sample'), may hold values from 64 to 128, as said below
- q_gain: float32 [128], replicated, may hold values from 0.5 to 4
- k_gain: float32 [128], replicated, may hold values from 0.5 to 4
- d_out: bfloat16 [4, 32, 128, 4096], P('prompt', 'sample', None, 'head'), may hold values from -6 to 6
Outputs:
- attn_out: bfloat16 [4, 32, 128, 4096], P('prompt', 'sample', None, 'head')
- d_q: bfloat16 [4, 32, 128, 4096], P('prompt', 'sample', None, 'head')
- d_comp_k: bfloat16 [4, 32, 128, 512], P('prompt', 'sample', None, 'head')
- d_comp_v: bfloat16 [4, 32, 128, 512], P('prompt', 'sample', None, 'head')
- d_prompt_k: bfloat16 [4, 3072, 512], P('prompt', 'sample', 'head')
- d_prompt_v: bfloat16 [4, 3072, 512], P('prompt', 'sample', 'head')
- gain_grads: float32 [2, 128], replicated
Inputs may be any that keep to these rules, and one draw needn't show every extreme that they name: `lengths`: multiples of 64; in every group one completion has 128 live tokens and another 64.
All inputs are finite; a program needn't handle non-finite values.
Results may differ from a plain program's by a relative error of at most 0.03.
Values may be sent and summed in bfloat16 or wider, within the bound.
A program may use at most 64 MiB of HBM per device.

v0:
```python
import math

import jax
import jax.numpy as jnp
from jax import lax
from jax.sharding import PartitionSpec as P

EPS = 1e-06


def normalize(inputs, gain_vec):
    inverse_rms = lax.rsqrt(jnp.mean(inputs * inputs, axis=-1, keepdims=True) + EPS)
    return inputs * inverse_rms * gain_vec


def normalize_back(inputs, gain_vec, upstream):
    _, pullback = jax.vjp(normalize, inputs, gain_vec)
    return pullback(upstream)


def per_device(comp_q, comp_k, comp_v, prompt_k, prompt_v, lengths, q_gain, k_gain, d_out):
    comp_len = comp_q.shape[2]
    q_width = comp_q.shape[3]
    head_dim = q_gain.shape[0]
    kv_local = comp_k.shape[3] // head_dim
    q_heads = q_width // head_dim
    group_size = q_heads // kv_local
    rows_own = prompt_k.shape[1]
    score_scale = 1.0 / math.sqrt(head_dim)
    live_count = lengths[0, 0]
    query_raw = comp_q[0, 0].astype(jnp.float32).reshape(comp_len, kv_local, group_size, head_dim)
    query_group = normalize(query_raw, q_gain).astype(jnp.bfloat16).transpose(1, 2, 0, 3)
    key_raw = comp_k[0, 0].astype(jnp.float32).reshape(comp_len, kv_local, head_dim)
    own_keys = normalize(key_raw, k_gain).astype(jnp.bfloat16)
    own_vals = comp_v[0, 0].reshape(comp_len, kv_local, head_dim)
    prompt_raw = prompt_k[0].astype(jnp.float32).reshape(rows_own, kv_local, head_dim)
    prompt_norm = normalize(prompt_raw, k_gain).astype(jnp.bfloat16)
    prompt_vals = prompt_v[0].reshape(rows_own, kv_local, head_dim)
    all_keys, all_vals = (
        lax.all_gather(prompt_norm, "sample", axis=0, tiled=True),
        lax.all_gather(prompt_vals, "sample", axis=0, tiled=True),
    )
    prompt = all_keys.shape[0]
    block_rows = math.gcd(prompt, 256)
    block_count = prompt // block_rows

    def in_blocks(values):
        return values.reshape(block_count, block_rows, kv_local, head_dim)

    def tile_logits(key_tile):
        return (
            jnp.einsum("kgqd,jkd->kgqj", query_group, key_tile, preferred_element_type=jnp.float32)
            * score_scale
        )

    row_ids = jnp.arange(comp_len, dtype=jnp.int32)
    causal = row_ids[None, :] <= row_ids[:, None]
    own_logits = jnp.where(causal, tile_logits(own_keys), -jnp.inf)
    row_max = jnp.max(own_logits, axis=-1)
    row_sum = jnp.sum(jnp.exp(own_logits - row_max[..., None]), axis=-1)

    def stat_step(state_in, key_block):
        old_max, old_sum = state_in
        logits = tile_logits(key_block)
        new_max = jnp.maximum(old_max, jnp.max(logits, axis=-1))
        new_sum = old_sum * jnp.exp(old_max - new_max) + jnp.sum(
            jnp.exp(logits - new_max[..., None]), axis=-1
        )
        return ((new_max, new_sum), logits)

    (row_max, row_sum), stored_logits = lax.scan(stat_step, (row_max, row_sum), in_blocks(all_keys))
    log_norm = (row_max + jnp.log(row_sum))[..., None]
    own_prob = jnp.exp(own_logits - log_norm).astype(jnp.bfloat16)
    mixture = jnp.einsum("kgqj,jkd->kgqd", own_prob, own_vals, preferred_element_type=jnp.float32)

    def mix_step(acc_mix, pair):
        logit_block, value_block = pair
        prob_tile = jnp.exp(logit_block - log_norm).astype(jnp.bfloat16)
        return (
            acc_mix
            + jnp.einsum(
                "kgqj,jkd->kgqd", prob_tile, value_block, preferred_element_type=jnp.float32
            ),
            None,
        )

    mixture, _ = lax.scan(mix_step, mixture, (stored_logits, in_blocks(all_vals)))
    live_rows = (row_ids < live_count)[None, None, :, None]
    attended = jnp.where(live_rows, mixture, 0.0).astype(jnp.bfloat16)
    grad_in = d_out[0, 0].reshape(comp_len, kv_local, group_size, head_dim).transpose(1, 2, 0, 3)
    grad_out = jnp.where(live_rows, grad_in, jnp.zeros_like(grad_in))
    row_dot = jnp.sum(grad_out.astype(jnp.float32) * attended.astype(jnp.float32), axis=-1)[
        ..., None
    ]

    def tile_grads(key_tile, value_tile, logits):
        attn_prob = jnp.exp(logits - log_norm)
        dprob = jnp.einsum(
            "kgqd,jkd->kgqj", grad_out, value_tile, preferred_element_type=jnp.float32
        )
        dlogit = (attn_prob * (dprob - row_dot)).astype(jnp.bfloat16)
        grad_query = (
            jnp.einsum("kgqj,jkd->kgqd", dlogit, key_tile, preferred_element_type=jnp.float32)
            * score_scale
        )
        grad_key = (
            jnp.einsum("kgqj,kgqd->jkd", dlogit, query_group, preferred_element_type=jnp.float32)
            * score_scale
        )
        grad_value = jnp.einsum(
            "kgqj,kgqd->jkd",
            attn_prob.astype(jnp.bfloat16),
            grad_out,
            preferred_element_type=jnp.float32,
        )
        return (grad_query, grad_key, grad_value)

    grad_query, own_dkey, own_dvalue = tile_grads(own_keys, own_vals, own_logits)

    def grad_step(acc_query, triple):
        key_block, value_block, logit_block = triple
        block_dq, block_dk, block_dv = tile_grads(key_block, value_block, logit_block)
        return (acc_query + block_dq, jnp.concatenate([block_dk, block_dv], axis=-1))

    grad_query, kv_terms = lax.scan(
        grad_step, grad_query, (in_blocks(all_keys), in_blocks(all_vals), stored_logits)
    )
    kv_terms = kv_terms.reshape(prompt, kv_local, 2 * head_dim)
    summed = lax.psum_scatter(
        kv_terms.astype(jnp.bfloat16), "sample", scatter_dimension=0, tiled=True
    ).astype(jnp.float32)
    dpk_raw, gain_k_prompt = normalize_back(prompt_raw, k_gain, summed[..., :head_dim])
    dq_raw, gain_q = normalize_back(query_raw, q_gain, grad_query.transpose(2, 0, 1, 3))
    dk_raw, gain_k_own = normalize_back(key_raw, k_gain, own_dkey)
    gain_terms = jnp.stack([gain_q, gain_k_own + gain_k_prompt])
    gain_total = lax.psum(gain_terms, ("prompt", "sample", "head"))
    row_count = (
        lax.axis_size("prompt")
        * lax.axis_size("sample")
        * comp_len
        * q_heads
        * lax.axis_size("head")
    )
    gain_grads = gain_total / math.sqrt(row_count)
    attn_out = attended.transpose(2, 0, 1, 3).reshape(1, 1, comp_len, q_width)
    d_q = dq_raw.astype(jnp.bfloat16).reshape(1, 1, comp_len, q_width)
    d_comp_k = dk_raw.astype(jnp.bfloat16).reshape(1, 1, comp_len, kv_local * head_dim)
    d_comp_v = own_dvalue.astype(jnp.bfloat16).reshape(1, 1, comp_len, kv_local * head_dim)
    d_prompt_k = dpk_raw.astype(jnp.bfloat16).reshape(1, rows_own, kv_local * head_dim)
    d_prompt_v = (
        summed[..., head_dim:].astype(jnp.bfloat16).reshape(1, rows_own, kv_local * head_dim)
    )
    return (attn_out, d_q, d_comp_k, d_comp_v, d_prompt_k, d_prompt_v, gain_grads)


def solution(mesh):
    return jax.shard_map(
        per_device,
        mesh=mesh,
        in_specs=(
            P("prompt", "sample", None, "head"),
            P("prompt", "sample", None, "head"),
            P("prompt", "sample", None, "head"),
            P("prompt", "sample", "head"),
            P("prompt", "sample", "head"),
            P("prompt", "sample"),
            P(),
            P(),
            P("prompt", "sample", None, "head"),
        ),
        out_specs=(
            P("prompt", "sample", None, "head"),
            P("prompt", "sample", None, "head"),
            P("prompt", "sample", None, "head"),
            P("prompt", "sample", None, "head"),
            P("prompt", "sample", "head"),
            P("prompt", "sample", "head"),
            P(),
        ),
        check_vma=False,
    )
```

profile of v0, /device:TPU:1, one launch (start us, length us, event | category | flops | bytes accessed | tf_op | source)
XLA Modules:
  0.0 446.0 jit_solution(5834227973111196748)
XLA Ops:
  12.1 47.6 %all_gather.6 = bf16[3072,1,128]{2,0,1:T(8,128)(2,1)} all-gather(bf16[96,1,128]{2,0,1:T(8,128)(2,1)S(1)} %fusion.74), channel_id=1, replica_groups=mesh['prompt'=4,'sample'=32,'head'=4] {'sample'}, dimensions={0}, use_global_device_ids=true | all-gather | bytes 811008 | tf_op jit(solution)/shard_map/all_gather | solution.py:40
  60.8 33.1 %while.36 = (s32[]{:T(128)}, f32[1,8,128]{2,1,0:T(8,128)S(1)}, f32[1,8,128]{2,1,0:T(8,128)S(1)}, f32[12,1,8,128,256]{4,3,2,1,0:T(8,128)}, bf16[12,256,1,128]{3,1...) while((s32[]{:T(128)}, f32[1,8,128]{2,1,0:T(8,128)S(1)}, f32[1,8,128]{2,1,0:T(8,128)S(1)}, ...), condition=%wide.region_8.9_spmd, body=%wide.region_5.8_spmd.sunk | while | flops 68159488 | bytes 6673485 | solution.py:71
  60.8 1.2 bitcast_reduce_fusion.2
  93.9 36.7 %all-gather = bf16[1,3072,128]{2,1,0:T(8,128)(2,1)} all-gather(bf16[1,96,128]{2,1,0:T(8,128)(2,1)S(1)} %copy-done.6), channel_id=2, replica_groups=mesh['prompt'=4,'sample'=32,'head'=4] {'sample'}, dimensions={1}, use_global_device_ids=true | all-gather | bytes 811008 | tf_op jit(solution)/shard_map/all_gather | solution.py:41
  130.9 19.5 %while.37 = (s32[]{:T(128)}, f32[1,8,128,128]{3,2,1,0:T(8,128)S(1)}, f32[12,1,8,128,256]{4,3,2,1,0:T(8,128)}, f32[1,8,128,1]{2,1,3,0:T(8,128)S(1)}, bf16[12,256,1,128]{3,1,2,0:T(8,128)(2,1)}, /*index=5*/s32[]{:T(128)}) while((s32[]{:T(128)}, f32[1,8,128,128]{3,2,1,0:T(8,128)S(1)}, f32[12,1,8,128,256]{4,3,2,1,0:T(8,128)}, ...), condition=%wide.region_10.11_spmd, body=%wide.region_9.10_spmd.sunk | while | flops 67764224 | bytes 2167877 | solution.py:87
  130.9 1.6 fusion.126
  132.5 1.6 fusion.126
  134.2 1.6 fusion.126
  135.8 1.6 fusion.126
  137.4 1.6 fusion.126
  139.0 1.6 fusion.126
  140.6 1.6 fusion.126
  142.3 1.6 fusion.126
  143.9 1.6 fusion.126
  145.5 1.6 fusion.126
  147.1 1.6 fusion.126
  148.8 1.6 fusion.126
  153.2 65.1 %while.38 = (s32[]{:T(128)}, f32[1,8,128,128]{3,2,1,0:T(8,128)S(1)}, bf16[12,256,1,256]{1,3,2,0:T(8,128)(2,1)}, f32[12,1,8,128,256]{4,3,2,1,0:T(8,128)}, f32[1,8...) while((s32[]{:T(128)}, ...), condition=%wide.region_13.14_spmd, body=%wide.region_12.13_spmd.sunk | while | flops 270598144 | bytes 10237553 | solution.py:125
  153.2 1.3 constant_dynamic-slice_fusion.2
  157.4 1.2 fusion.136
  158.6 1.3 constant_dynamic-slice_fusion.2
  162.8 1.2 fusion.136
  164.0 1.3 constant_dynamic-slice_fusion.2
  168.2 1.2 fusion.136
  169.5 1.3 constant_dynamic-slice_fusion.2
  173.7 1.2 fusion.136
  174.9 1.3 constant_dynamic-slice_fusion.2
  179.1 1.2 fusion.136
  180.3 1.3 constant_dynamic-slice_fusion.2
  185.8 1.3 constant_dynamic-slice_fusion.2
  190.0 1.2 fusion.136
  191.2 1.3 constant_dynamic-slice_fusion.2
  195.4 1.2 fusion.136
  196.6 1.3 constant_dynamic-slice_fusion.2
  202.1 1.3 constant_dynamic-slice_fusion.2
  206.3 1.2 fusion.136
  207.5 1.3 constant_dynamic-slice_fusion.2
  211.7 1.2 fusion.136
  212.9 1.3 constant_dynamic-slice_fusion.2
  217.1 1.2 fusion.136
  218.3 2.6 copy.70
  221.2 1.3 fusion.65
  224.6 1.8 copy.88
  226.3 1.4 fusion.39
  228.4 105.9 %reduce-scatter.2.cloned.1.call-done = bf16[96,1,256]{2,0,1:T(8,128)(2,1)} async-done(((bf16[3072,1,256]{2,0,1:T(8,128)(2,1)}), bf16[96,1,256]{2,0,1:T(8,128)(2,1)}) %reduce-scatter.2.cloned.1.call-update) | async-done | bytes 49168 | tf_op jit(solution)/shard_map/reduce_scatter | solution.py:129
  335.3 100.5 %psum.7 = f32[2,128]{1,0:T(2,128)S(1)} all-reduce(f32[2,128]{1,0:T(2,128)S(1)} %pad_maximum_fusion), channel_id=1, replica_groups=mesh['prompt'=4,'sample'=32,'head'=4] {'prompt','sample','head'}, use_global_device_ids=true, to_apply=%region_21.22 | all-reduce | flops 256 | bytes 2048 | tf_op jit(solution)/shard_map/psum | solution.py:136
  436.3 1.4 slice_bitcast_fusion
  437.7 1.4 fusion.90
  (213 shorter events, 80.7 us)
Async XLA Ops:
  7.2 123.5 %copy-start = (bf16[1,1,128,128]{3,2,1,0:T(8,128)(2,1)S(1)}, bf16[1,1,128,128]{3,2,1,0:T(8,128)(2,1)}, u32[]{:S(2)}) copy-start(bf16[1,1,128,128]{3,2,1,0:T(8,128)(2,1)} %param.17) | copy-start | bytes 98308
  7.2 327.1 %reduce-scatter.2.cloned.1.call-start = ((), (), s32[]{:S(2)}) async-start(), calls=%async_computation.1 | async-start | bytes 1622016 | tf_op jit(solution)/shard_map/reduce_scatter | solution.py:129
  9.4 51.4 %copy-start.9 = (f32[128]{0:T(128)}, f32[128]{0:T(128)S(1)}, u32[]{:S(2)}) copy-start(f32[128]{0:T(128)S(1)} %fusion.62) | copy-start | bytes 1540
  11.2 49.6 %copy-start.11 = (f32[96]{0:T(128)}, f32[96]{0:T(128)S(1)}, u32[]{:S(2)}) copy-start(f32[96]{0:T(128)S(1)} %fusion.77) | copy-start | bytes 1156
  60.7 91.6 %copy-start.1 = (f32[8,128,128]{1,2,0:T(8,128)}, f32[8,128,128]{1,2,0:T(8,128)S(1)}, u32[]{:S(2)}) copy-start(f32[8,128,128]{1,2,0:T(8,128)S(1)} %get-tuple-element.239) | copy-start | bytes 1572868
  60.8 33.2 %copy-start.6 = (bf16[1,96,128]{2,1,0:T(8,128)(2,1)S(1)}, bf16[1,96,128]{2,1,0:T(8,128)(2,1)}, u32[]{:S(2)}) copy-start(bf16[1,96,128]{2,1,0:T(8,128)(2,1)} %param.19) | copy-start | bytes 73732
  93.9 56.6 %copy-start.5 = (bf16[1,1,128,1024]{3,2,1,0:T(8,128)(2,1)S(1)}, bf16[1,1,128,1024]{3,2,1,0:T(8,128)(2,1)}, u32[]{:S(2)}) copy-start(bf16[1,1,128,1024]{3,2,1,0:T(8,128)(2,1)} %param.23) | copy-start | bytes 786436
  93.9 58.6 %copy-start.7 = (f32[128]{0:T(128)S(1)}, f32[128]{0:T(128)}, u32[]{:S(2)}) copy-start(f32[128]{0:T(128)} %param.22) | copy-start | bytes 1540
  150.7 2.3 copy-start.2
  152.5 0.7 copy-start.3
  153.0 68.2 %copy-start.8 = (f32[128]{0:T(128)S(1)}, f32[128]{0:T(128)}, u32[]{:S(2)}) copy-start(f32[128]{0:T(128)} %param.21) | copy-start | bytes 1540
  153.0 69.5 %copy-start.10 = (f32[128]{0:T(128)S(1)}, f32[128]{0:T(128)}, u32[]{:S(2)}) copy-start(f32[128]{0:T(128)} %copy-done.9) | copy-start | bytes 1540
  153.0 181.3 %copy-start.4 = (bf16[1,96,128]{2,1,0:T(8,128)(2,1)S(1)}, bf16[1,96,128]{2,1,0:T(8,128)(2,1)}, u32[]{:S(2)}) copy-start(bf16[1,96,128]{2,1,0:T(8,128)(2,1)} %param.18) | copy-start | bytes 73732
  153.0 283.3 %copy-start.12 = (f32[96]{0:T(128)S(1)}, f32[96]{0:T(128)}, u32[]{:S(2)}) copy-start(f32[96]{0:T(128)} %copy-done.11) | copy-start | bytes 1156
Sparse Core Ops, SparseCore 0:
  221.1 113.1 reduce-scatter.1
where the time goes:
time: 449 us; the launch traced here: 446 us
  blocking collectives  185 us (41%)
  waiting for transfers between devices  106 us (24%)
  matrix products  74 us (16%)
  local copies, waits for them, and re-layouts  47.9 us (11%)
  other arithmetic  17 us (4%)
  between operations  15.1 us (3%)
    reduce_scatter x1, waiting for transfers between devices, per_device(): lax.psum_scatter(kv_terms.astype(jnp.bfloat16), 'sample', scatter_dimensi...  106 us
    psum x1, blocking collectives, per_device(): gain_total = lax.psum(gain_terms, ('prompt', 'sample', 'head'))  100 us
    all_gather x1, blocking collectives, per_device(): lax.all_gather(prompt_norm, 'sample', axis=0, tiled=True)  47.6 us
    all_gather x1, blocking collectives, per_device(): lax.all_gather(prompt_vals, 'sample', axis=0, tiled=True)  36.7 us
    dynamic_slice x24, local copies, waits for them, and re-layouts, per_device(): lax.scan(mix_step, mixture, (stored_logits, in_blocks(all_vals)))  19.9 us
    dot_general x12, matrix products, mix_step(): jnp.einsum('kgqj,jkd->kgqd', prob_tile, value_block, preferred_element_ty...  19.2 us
    dynamic_update_slice x24, local copies, waits for them, and re-layouts, per_device(): lax.scan(stat_step, (row_max, row_sum), in_blocks(all_keys))  16.8 us
    dot_general x13, matrix products, tile_logits(): jnp.einsum('kgqd,jkd->kgqj', query_group, key_tile, preferred_element_typ...  14.8 us
  transfers between devices with their start and end apart: 1, of which 1 were waited for; matrix products, arithmetic and copies ran while one was open for 2% of the time, Pallas kernels for 0%

commit v1 on v0

v1 whole, which is shorter than its diff:
```python
import functools
import math

import jax
import jax.numpy as jnp
from jax import lax
from jax.experimental import pallas as pl
from jax.experimental.pallas import tpu as pltpu
from jax.sharding import PartitionSpec as P

EPS = 1e-06
BF = jnp.bfloat16
F32 = jnp.float32
NT = (((1,), (1,)), ((), ()))
NN = (((1,), (0,)), ((), ()))
DH = 128
TOK = 128
QH = 8
NQ = TOK * QH
Q2 = 2 * NQ
OWN = 96
GR = 4 * OWN
NG = 4
KEYS = NG * GR
QB = 256
SCALE = 1.0 / math.sqrt(DH)
C2 = SCALE / math.log(2.0)
LOW = -1e30
MESH = pl.DeviceIdType.MESH


def dot(a, b, dims):
    return lax.dot_general(a, b, dims, preferred_element_type=F32)


def rms(x):
    return lax.rsqrt(jnp.mean(x * x, axis=-1, keepdims=True) + EPS)


def norm_back(x, gain, up):
    r = rms(x)
    g = up * gain
    return r * g - x * (r * r * r * jnp.mean(x * g, axis=-1, keepdims=True))


def row_near(d):
    return ((d - 1) * 4 + 2) * OWN


def row_far(d):
    return d * 4 * OWN


ROW_FAR0 = OWN
ROW_FAR4 = (3 * 4 + 3) * OWN


def kernel(
    cq, ck, cv, pk, pv, live_ref, q_gain, k_gain, d_out,
    out, dq, dck, dcv, dpk, dpv, gains,
    kv, q, do, ownkv, trans, s_buf, e_buf, dp_buf, e_own, dp_own, o_t, dq_t, o_rem, dq_rem, m_run,
    m_at, stat, stat_rem, fac, part, y_out, y_in, y4_out, y4_in, z_out, z_in, g_acc, g_buf,
    zp_s, zp_r, zm_s, zm_r, y_s, y_r, c_s, c_r, ry_s, ry_r, rp_s, rp_r, rm_s, rm_r, g_s, g_r,
):
    sample = lax.axis_index("sample")
    px = lax.axis_index("prompt")
    hy = lax.axis_index("head")
    core = lax.rem(sample, 2)
    y = lax.rem(sample // 2, 2)
    z = sample // 4

    def at(z_, y_, c_):
        return z_ * 4 + y_ * 2 + c_

    sib = {"sample": at(z, y, 1 - core)}
    ynb = {"sample": at(z, 1 - y, core)}
    zup = {"sample": at(lax.rem(z + 1, 8), y, core)}
    zdn = {"sample": at(lax.rem(z + 7, 8), y, core)}

    my_slot = (px * 2 + core, z, hy * 2 + y)

    def partner(r, i):
        if r == 0:
            return {"prompt": i // 2, "sample": at(z, y, lax.rem(i, 2))}
        if r == 1:
            return {"sample": at(i, y, core)}
        return {"head": i // 2, "sample": at(z, lax.rem(i, 2), core)}

    def send(src, dst, ss, rs, dev):
        return pltpu.make_async_remote_copy(
            src_ref=src, dst_ref=dst, send_sem=ss, recv_sem=rs, device_id=dev, device_id_type=MESH
        )

    barrier = pltpu.get_barrier_semaphore()
    for r in range(3):
        for k in range(1, 8):
            pl.semaphore_signal(
                barrier, inc=1, device_id=partner(r, lax.rem(my_slot[r] + k, 8)), device_id_type=MESH
            )

    kg = k_gain[...]
    qg = q_gain[...]
    pk_raw = pk[...].astype(F32)
    kv[0:OWN, 0:DH] = (pk_raw * rms(pk_raw) * kg).astype(BF)
    kv[0:OWN, DH:] = pv[...]
    pl.semaphore_wait(barrier, 21)

    def rows(start, count=OWN):
        return kv.at[pl.ds(start, count), :]

    def copy_zp(d, src):
        return send(rows(src), rows(row_near(d)), zp_s.at[d - 1], zp_r.at[d - 1], zdn)

    def copy_zm(d, src):
        return send(rows(src), rows(row_near(d) + OWN), zm_s.at[d - 1], zm_r.at[d - 1], zup)

    def copy_y(i, src, dst):
        return send(rows(src), rows(dst), y_s.at[i], y_r.at[i], ynb)

    copy_zp(1, 0).start()
    copy_zm(1, 0).start()
    copy_y(0, 0, ROW_FAR0).start()

    live = live_ref[0, 0]
    live_rows = lax.broadcasted_iota(jnp.int32, (TOK, 1), 0) < live
    for h in range(QH):
        x = cq[:, h * DH : (h + 1) * DH].astype(F32)
        q[h * TOK : (h + 1) * TOK, :] = (x * rms(x) * qg).astype(BF)
        g = d_out[:, h * DH : (h + 1) * DH]
        do[h * TOK : (h + 1) * TOK, :] = jnp.where(live_rows, g, jnp.zeros_like(g))
    copy_q = send(q.at[0:NQ, :], q.at[NQ:, :], c_s.at[0], c_r.at[0], sib)
    copy_do = send(do.at[0:NQ, :], do.at[NQ:, :], c_s.at[1], c_r.at[1], sib)
    copy_q.start()
    copy_do.start()

    ck_raw = ck[...].astype(F32)
    ownkv[:, 0:DH] = (ck_raw * rms(ck_raw) * kg).astype(BF)
    ownkv[:, DH:] = cv[...]

    m_run[...] = jnp.full((1, Q2), LOW, F32)
    stat[...] = jnp.zeros((8, Q2), F32)
    o_t[:, NQ:] = jnp.zeros((DH, NQ), F32)
    own_v_t = ownkv[:, DH:].astype(F32).T.astype(BF)
    trans[:, 0:TOK] = own_v_t
    u_ids = lax.broadcasted_iota(jnp.int32, (TOK, QB), 0)
    t_ids = lax.rem(lax.broadcasted_iota(jnp.int32, (TOK, QB), 1), TOK)
    allowed = u_ids <= t_ids
    for b in range(NQ // QB):
        sl = slice(b * QB, (b + 1) * QB)
        s = jnp.where(allowed, dot(ownkv[:, 0:DH], q[sl, :], NT), LOW)
        dp = dot(ownkv[:, DH:], do[sl, :], NT)
        m = jnp.max(s, axis=0, keepdims=True)
        e = jnp.exp2((s - m) * C2)
        eb = e.astype(BF)
        e_own[:, sl] = eb
        dp_own[:, sl] = dp
        m_run[:, sl] = m
        stat[1:2, sl] = jnp.sum(e, axis=0, keepdims=True)
        stat[2:3, sl] = jnp.sum(e * dp, axis=0, keepdims=True)
        o_t[:, sl] = dot(trans[:, 0:TOK], eb, NN)
    m_at[NG] = m_run[...]

    copy_q.wait_recv()
    copy_do.wait_recv()

    def forward(g, carry):
        near = row_near(g + 1)
        copy_zp(g + 1, near).wait_recv()

        @pl.when(g < 3)
        def _():
            copy_zp(g + 2, near).start()
            copy_y(g + 1, near, row_far(g + 1)).start()
            copy_zm(g + 1, near).wait_recv()
            copy_y(g + 4, near + OWN, row_far(g + 1) + OWN).start()

        @pl.when(g < 2)
        def _():
            copy_zm(g + 2, near + OWN).start()

        @pl.when(g == 3)
        def _():
            copy_y(7, near, ROW_FAR4).start()

        @pl.when(g == 0)
        def _():
            copy_y(0, 0, ROW_FAR0).wait_recv()

        @pl.when(g > 0)
        def _():
            copy_y(g, 0, row_far(g)).wait_recv()
            copy_y(g + 3, 0, row_far(g) + OWN).wait_recv()

        @pl.when(g == 3)
        def _():
            copy_y(7, 0, ROW_FAR4).wait_recv()

        at_rows = pl.ds(pl.multiple_of(g * GR, GR), GR)
        keys = kv[at_rows, 0:DH]
        vals = kv[at_rows, DH:]
        trans[...] = vals.astype(F32).T.astype(BF)
        tiles = Q2 // QB
        mx, al, mc, zs, ds = {}, {}, {}, {}, {}

        def sl(b):
            return slice(b * QB, (b + 1) * QB)

        for t in range(tiles + 2):
            if 1 <= t <= tiles:
                b = t - 1
                m_old = m_run[:, sl(b)]
                m_new = jnp.maximum(m_old, mx[b])
                m_run[:, sl(b)] = m_new
                al[b] = jnp.exp2((m_old - m_new) * C2)
                mc[b] = m_new * C2
            if t < tiles:
                s = dot(keys, q[sl(t), :], NT)
                s_buf[:, sl(t)] = s
                mx[t] = jnp.max(s, axis=0, keepdims=True)
                dp_buf[at_rows, sl(t)] = dot(vals, do[sl(t), :], NT)
            if 1 <= t <= tiles:
                b = t - 1
                e = jnp.exp2(s_buf[:, sl(b)] * C2 - mc[b])
                e_buf[at_rows, sl(b)] = e.astype(BF)
                stat[1:2, sl(b)] = stat[1:2, sl(b)] * al[b] + jnp.sum(e, axis=0, keepdims=True)
                stat[2:3, sl(b)] = stat[2:3, sl(b)] * al[b] + jnp.sum(
                    e * dp_buf[at_rows, sl(b)], axis=0, keepdims=True
                )
            if t >= 2:
                b = t - 2
                o_t[:, sl(b)] = o_t[:, sl(b)] * al[b] + dot(trans[...], e_buf[at_rows, sl(b)], NN)
        m_at[g] = m_run[...]
        return carry

    lax.fori_loop(0, NG, forward, 0)

    stat[0:1, :] = m_run[...]
    copy_st = send(stat, stat_rem, c_s.at[2], c_r.at[2], sib)
    copy_st.start()
    dq_t[...] = jnp.zeros((DH, Q2), F32)
    g_acc[...] = jnp.zeros((8, DH), F32)
    z_in[3, OWN:, :] = jnp.zeros((OWN, 2 * DH), BF)
    copy_st.wait_recv()
    for half in range(2):
        mine = slice(half * NQ, (half + 1) * NQ)
        other = slice((1 - half) * NQ, (2 - half) * NQ)
        m_a, m_b = stat[0:1, mine], stat_rem[0:1, other]
        m_f = jnp.maximum(m_a, m_b)
        w_a, w_b = jnp.exp2((m_a - m_f) * C2), jnp.exp2((m_b - m_f) * C2)
        inv = 1.0 / (stat[1:2, mine] * w_a + stat_rem[1:2, other] * w_b)
        for i in range(NG + (1 - half)):
            fac[i, :, mine] = jnp.exp2((m_at[i, :, mine] - m_f) * C2) * inv
        fac[NG + 1, :, mine] = (stat[2:3, mine] * w_a + stat_rem[2:3, other] * w_b) * inv
        o_t[:, mine] = o_t[:, mine] * (w_a * inv)
    copy_o = send(o_t.at[:, NQ:], o_rem, c_s.at[3], c_r.at[3], sib)
    copy_o.start()

    def copy_ry(g):
        return send(y_out.at[g], y_in.at[g], ry_s.at[g], ry_r.at[g], ynb)

    copy_ry0 = send(y_out.at[0, OWN:, :], y_in.at[0, OWN:, :], ry_s.at[0], ry_r.at[0], ynb)
    copy_ry4 = send(y4_out, y4_in, ry_s.at[4], ry_r.at[4], ynb)

    def copy_rp(g):
        return send(z_out.at[g, 0:OWN, :], z_in.at[g, 0:OWN, :], rp_s.at[g], rp_r.at[g], zup)

    def copy_rm(g):
        return send(z_out.at[g, OWN:, :], z_in.at[g, OWN:, :], rm_s.at[g], rm_r.at[g], zdn)

    def backward(i, carry):
        g = NG - 1 - i
        at_rows = pl.ds(pl.multiple_of(g * GR, GR), GR)
        keys = kv[at_rows, 0:DH]
        trans[...] = keys.astype(F32).T.astype(BF)
        dk = jnp.zeros((GR, DH), F32)
        dv = jnp.zeros((GR, DH), F32)
        for b in range(Q2 // QB):
            sl = slice(b * QB, (b + 1) * QB)
            p = e_buf[at_rows, sl].astype(F32) * fac[g, :, sl]
            pb = p.astype(BF)
            ds = (p * (dp_buf[at_rows, sl] - fac[NG + 1, :, sl])).astype(BF)
            dv = dv + dot(pb, do[sl, :], NN)
            dk = dk + dot(ds, q[sl, :], NN)
            dq_t[:, sl] += dot(trans[...], ds, NN)
        part[:, 0:DH] = dk
        part[:, DH:] = dv
        g_acc[...] += jnp.sum((dk * keys.astype(F32)).reshape(GR // 8, 8, DH), axis=0)

        y_out[g] = part[0 : 2 * OWN, :].astype(BF)

        @pl.when(g > 0)
        def _():
            copy_ry(g).start()

        @pl.when(g == 0)
        def _():
            copy_ry0.start()

        @pl.when(g == 3)
        def _():
            y4_out[...] = part[3 * OWN :, :].astype(BF)
            copy_ry4.start()
            copy_ry4.wait_recv()
            z_out[3, 0:OWN, :] = (part[2 * OWN : 3 * OWN, :] + y4_in[...].astype(F32)).astype(BF)
            copy_rp(3).start()

        @pl.when(g < 3)
        def _():
            copy_ry(g + 1).wait_recv()
            copy_rp(g + 1).wait_recv()

            @pl.when(g < 2)
            def _():
                copy_rm(g + 1).wait_recv()

            z_out[g] = (
                part[2 * OWN :, :] + y_in[g + 1].astype(F32) + z_in[g + 1].astype(F32)
            ).astype(BF)
            copy_rp(g).start()
            copy_rm(g).start()

        return carry

    lax.fori_loop(0, NG, backward, 0)

    copy_dq = send(dq_t.at[:, NQ:], dq_rem, c_s.at[4], c_r.at[4], sib)
    copy_dq.start()

    trans[:, 0:TOK] = ownkv[:, 0:DH].astype(F32).T.astype(BF)
    dk = jnp.zeros((TOK, DH), F32)
    dv = jnp.zeros((TOK, DH), F32)
    for b in range(NQ // QB):
        sl = slice(b * QB, (b + 1) * QB)
        p = e_own[:, sl].astype(F32) * fac[NG, :, sl]
        pb = p.astype(BF)
        ds = (p * (dp_own[:, sl] - fac[NG + 1, :, sl])).astype(BF)
        dv = dv + dot(pb, do[sl, :], NN)
        dk = dk + dot(ds, q[sl, :], NN)
        dq_t[:, sl] += dot(trans[:, 0:TOK], ds, NN)
    g_part = g_acc[...] + jnp.sum(
        (dk * ownkv[:, 0:DH].astype(F32)).reshape(TOK // 8, 8, DH), axis=0
    )

    def g_copy(r, i, dev):
        return send(g_buf.at[r, i], g_buf.at[r, i], g_s.at[r, i], g_r.at[r, i], dev)

    def g_start(r, value):
        g_buf[r, my_slot[r]] = value
        for k in range(1, 8):
            j = lax.rem(my_slot[r] + k, 8)
            pltpu.make_async_remote_copy(
                src_ref=g_buf.at[r, my_slot[r]],
                dst_ref=g_buf.at[r, my_slot[r]],
                send_sem=g_s.at[r, k],
                recv_sem=g_r.at[r, my_slot[r]],
                device_id=partner(r, j),
                device_id_type=MESH,
            ).start()

    def g_wait(r):
        for k in range(1, 8):
            j = lax.rem(my_slot[r] + k, 8)
            send(
                g_buf.at[r, j], g_buf.at[r, j], g_s.at[r, k], g_r.at[r, j], partner(r, j)
            ).wait_recv()
        total = g_buf[r, 0]
        for k in range(1, 8):
            total = total + g_buf[r, k]
        return total

    g_start(0, g_part)
    dck[...] = norm_back(ck_raw, kg, dk * SCALE).astype(BF)
    dcv[...] = dv.astype(BF)

    copy_o.wait_recv()
    for h in range(QH // 2):
        sl = slice(h * TOK, (h + 1) * TOK)
        x = (o_t[:, sl] + o_rem[:, sl]).T
        out[:, h * DH : (h + 1) * DH] = jnp.where(live_rows, x, 0.0).astype(BF)
    g_start(1, g_wait(0))
    for h in range(QH // 2, QH):
        sl = slice(h * TOK, (h + 1) * TOK)
        x = (o_t[:, sl] + o_rem[:, sl]).T
        out[:, h * DH : (h + 1) * DH] = jnp.where(live_rows, x, 0.0).astype(BF)

    copy_ry0.wait_recv()
    copy_rp(0).wait_recv()
    copy_rm(0).wait_recv()
    z0 = z_in[0].astype(F32)
    total = part[0:OWN, :] + y_in[0, OWN:, :].astype(F32) + z0[0:OWN] + z0[OWN:]
    dpk[...] = norm_back(pk_raw, kg, total[:, 0:DH] * SCALE).astype(BF)
    dpv[...] = total[:, DH:].astype(BF)
    g_start(2, g_wait(1))

    copy_dq.wait_recv()
    for h in range(QH):
        sl = slice(h * TOK, (h + 1) * TOK)
        up = (dq_t[:, sl] + dq_rem[:, sl]).T * SCALE
        x = cq[:, h * DH : (h + 1) * DH].astype(F32)
        dq[:, h * DH : (h + 1) * DH] = norm_back(x, qg, up).astype(BF)

    g_sum = jnp.sum(g_wait(2), axis=0, keepdims=True) * (SCALE / math.sqrt(GAIN_ROWS))
    gains[0:1, :] = g_sum / qg
    gains[1:2, :] = g_sum / kg

    for d in range(1, 5):
        copy_zp(d, 0).wait_send()
    for d in range(1, 4):
        copy_zm(d, 0).wait_send()
    for i in range(8):
        copy_y(i, 0, 0).wait_send()
    copy_q.wait_send()
    copy_do.wait_send()
    copy_st.wait_send()
    copy_o.wait_send()
    copy_dq.wait_send()
    copy_ry0.wait_send()
    copy_ry4.wait_send()
    for g in range(1, NG):
        copy_ry(g).wait_send()
    for g in range(NG):
        copy_rp(g).wait_send()
    for g in range(NG - 1):
        copy_rm(g).wait_send()
    for r in range(3):
        for k in range(1, 8):
            j = lax.rem(my_slot[r] + k, 8)
            send(
                g_buf.at[r, my_slot[r]], g_buf.at[r, my_slot[r]], g_s.at[r, k], g_r.at[r, j], partner(r, j)
            ).wait_send()


GAIN_ROWS = 524288


def per_device(comp_q, comp_k, comp_v, prompt_k, prompt_v, lengths, q_gain, k_gain, d_out):
    vmem = pl.BlockSpec(memory_space=pltpu.VMEM)
    smem = pl.BlockSpec(memory_space=pltpu.SMEM)
    dma = pltpu.SemaphoreType.DMA
    width = QH * DH
    shapes = [
        jax.ShapeDtypeStruct((TOK, width), BF),
        jax.ShapeDtypeStruct((TOK, width), BF),
        jax.ShapeDtypeStruct((TOK, DH), BF),
        jax.ShapeDtypeStruct((TOK, DH), BF),
        jax.ShapeDtypeStruct((OWN, DH), BF),
        jax.ShapeDtypeStruct((OWN, DH), BF),
        jax.ShapeDtypeStruct((2, DH), F32),
    ]
    scratch = [
        pltpu.VMEM((KEYS, 2 * DH), BF),
        pltpu.VMEM((Q2, DH), BF),
        pltpu.VMEM((Q2, DH), BF),
        pltpu.VMEM((TOK, 2 * DH), BF),
        pltpu.VMEM((DH, GR), BF),
        pltpu.VMEM((GR, Q2), F32),
        pltpu.VMEM((KEYS, Q2), BF),
        pltpu.VMEM((KEYS, Q2), F32),
        pltpu.VMEM((TOK, NQ), BF),
        pltpu.VMEM((TOK, NQ), F32),
        pltpu.VMEM((DH, Q2), F32),
        pltpu.VMEM((DH, Q2), F32),
        pltpu.VMEM((DH, NQ), F32),
        pltpu.VMEM((DH, NQ), F32),
        pltpu.VMEM((1, Q2), F32),
        pltpu.VMEM((NG + 1, 1, Q2), F32),
        pltpu.VMEM((8, Q2), F32),
        pltpu.VMEM((8, Q2), F32),
        pltpu.VMEM((NG + 2, 1, Q2), F32),
        pltpu.VMEM((GR, 2 * DH), F32),
        pltpu.VMEM((NG, 2 * OWN, 2 * DH), BF),
        pltpu.VMEM((NG, 2 * OWN, 2 * DH), BF),
        pltpu.VMEM((OWN, 2 * DH), BF),
        pltpu.VMEM((OWN, 2 * DH), BF),
        pltpu.VMEM((NG, 2 * OWN, 2 * DH), BF),
        pltpu.VMEM((NG, 2 * OWN, 2 * DH), BF),
        pltpu.VMEM((8, DH), F32),
        pltpu.VMEM((3, 8, 8, DH), F32),
        dma((4,)), dma((4,)), dma((3,)), dma((3,)), dma((8,)), dma((8,)), dma((5,)), dma((5,)),
        dma((5,)), dma((5,)), dma((4,)), dma((4,)), dma((4,)), dma((4,)), dma((3, 8)), dma((3, 8)),
    ]
    res = pl.pallas_call(
        kernel,
        out_shape=shapes,
        in_specs=[vmem] * 5 + [smem] + [vmem] * 3,
        out_specs=[vmem] * 7,
        scratch_shapes=scratch,
        compiler_params=pltpu.CompilerParams(
            collective_id=0, has_side_effects=True, vmem_limit_bytes=56 * 2**20
        ),
    )(
        comp_q.reshape(TOK, width),
        comp_k.reshape(TOK, DH),
        comp_v.reshape(TOK, DH),
        prompt_k.reshape(OWN, DH),
        prompt_v.reshape(OWN, DH),
        lengths,
        q_gain.reshape(1, DH),
        k_gain.reshape(1, DH),
        d_out.reshape(TOK, width),
    )
    return (
        res[0].reshape(1, 1, TOK, width),
        res[1].reshape(1, 1, TOK, width),
        res[2].reshape(1, 1, TOK, DH),
        res[3].reshape(1, 1, TOK, DH),
        res[4].reshape(1, OWN, DH),
        res[5].reshape(1, OWN, DH),
        res[6],
    )


def solution(mesh):
    return jax.shard_map(
        per_device,
        mesh=mesh,
        in_specs=(
            P("prompt", "sample", None, "head"),
            P("prompt", "sample", None, "head"),
            P("prompt", "sample", None, "head"),
            P("prompt", "sample", "head"),
            P("prompt", "sample", "head"),
            P("prompt", "sample"),
            P(),
            P(),
            P("prompt", "sample", None, "head"),
        ),
        out_specs=(
            P("prompt", "sample", None, "head"),
            P("prompt", "sample", None, "head"),
            P("prompt", "sample", None, "head"),
            P("prompt", "sample", None, "head"),
            P("prompt", "sample", "head"),
            P("prompt", "sample", "head"),
            P(),
        ),
        check_vma=False,
    )
```

time: 449 us -> 74.6 us (0.17)
  blocking collectives: 185 us -> 0 us
  waiting for transfers between devices: 106 us -> 0 us
  matrix products: 74 us -> 0 us
  Pallas kernels: 0 us -> 66.8 us
  local copies, waits for them, and re-layouts: 47.9 us -> 5.97 us
  other arithmetic: 17 us -> 0 us
  between operations: 15.1 us -> 1.31 us
    reduce_scatter x1 -> x0, waiting for transfers between devices: 106 us -> none  [per_device(): lax.psum_scatter(kv_terms.astype(jnp.bfloat16), 'sample', scatter_dimensi...]
    psum x1 -> x0, blocking collectives: 100 us -> none  [per_device(): gain_total = lax.psum(gain_terms, ('prompt', 'sample', 'head'))]
    all_gather x2 -> x0, blocking collectives: 84.3 us -> none  [the longest x1 47.6 us: per_device(): lax.all_gather(prompt_norm, 'sample', axis=0, tiled=True)]
    dot_general x78 -> x0, matrix products: 74 us -> none  [the longest x12 19.2 us: mix_step(): jnp.einsum('kgqj,jkd->kgqd', prob_tile, value_block, preferred_element_ty...]
    pallas_call x0 -> x1, Pallas kernels: none -> 66.8 us  [per_device(): pl.pallas_call(kernel, out_shape=shapes, in_specs=[vmem] * 5 + [smem] + [...]
    dynamic_slice x24 -> x0, local copies, waits for them, and re-layouts: 19.9 us -> none  [per_device(): lax.scan(mix_step, mixture, (stored_logits, in_blocks(all_vals)))]
    dynamic_update_slice x24 -> x0, local copies, waits for them, and re-layouts: 16.8 us -> none  [per_device(): lax.scan(stat_step, (row_max, row_sum), in_blocks(all_keys))]
    dynamic_update_slice x12 -> x0, other arithmetic: 7.95 us -> none  [per_device(): lax.scan(grad_step, grad_query, (in_blocks(all_keys), in_blocks(all_vals)...]
  transfers between devices with their start and end apart: 1 -> 0, of which waited for: 1 -> 0; matrix products, arithmetic and copies ran while one was open for 2% -> 0% of each run, Pallas kernels for 0% -> 0%
where the time goes in v1:
time: 74.6 us; the launch traced here: 74.1 us
  Pallas kernels  66.8 us (90%)
  local copies, waits for them, and re-layouts  5.97 us (8%)
  between operations  1.31 us (2%)
    pallas_call x1, Pallas kernels, per_device(): pl.pallas_call(kernel, out_shape=shapes, in_specs=[vmem] * 5 + [smem] + [...  66.8 us
    unnamed x19, local copies, waits for them, and re-layouts  5.97 us

profile of v1, /device:TPU:1, one launch (start us, length us, event | category | flops | bytes accessed | tf_op | source)
XLA Modules:
  0.0 74.1 jit_solution(1181252997780246410)
XLA Ops:
  1.3 66.8 %shard_map.144 = (bf16[128,1024]{1,0:T(8,128)(2,1)}, bf16[128,1024]{1,0:T(8,128)(2,1)}, bf16[128,128]{1,0:T(8,128)(2,1)}, bf16[128,128]{1,0:T(8,128)(2,1)}, bf16...) custom-call(bf16[128,1024]{1,0:T(8,128)(2,1)} %bitcast.14, bf16[128,128]{1,0:T(8,128)(2,1)} %bitcast.18, ...), custom_call_target="tpu_custom_call" | custom-call | tf_op jit(solution)/shard_map/pallas_call | solution.py:482
  68.1 0.0 copy-start
  68.1 1.7 %copy.24 = bf16[1,1,128,1024]{3,2,1,0:T(8,128)(2,1)} copy(bf16[1,1,128,1024]{3,2,1,0:T(8,128)(2,1)} %bitcast.17) | data formatting | bytes 524288
  69.8 0.0 copy-done
  69.8 0.0 copy-start.2
  69.8 0.7 copy.25
  70.5 0.1 copy-done.2
  70.6 0.0 copy-start.1
  70.6 0.6 copy.26
  71.2 0.2 copy-done.1
  71.4 0.0 copy-start.4
  71.4 0.6 copy.27
  72.0 0.1 copy-done.4
  72.1 0.0 copy-start.3
  72.1 0.6 copy.28
  72.7 0.1 copy-done.3
  72.9 0.0 copy-start.5
  72.9 0.6 copy.29
  73.5 0.1 copy-done.5
  73.5 0.6 copy.30
Async XLA Ops:
  68.1 1.7 %copy-start = (bf16[128,1024]{1,0:T(8,128)(2,1)S(1)}, bf16[128,1024]{1,0:T(8,128)(2,1)}, u32[]{:S(2)}) copy-start(bf16[128,1024]{1,0:T(8,128)(2,1)} %get-tuple-element.15) | copy-start | bytes 786436
  69.8 0.8 %copy-start.2 = (bf16[128,128]{1,0:T(8,128)(2,1)S(1)}, bf16[128,128]{1,0:T(8,128)(2,1)}, u32[]{:S(2)}) copy-start(bf16[128,128]{1,0:T(8,128)(2,1)} %get-tuple-element.16) | copy-start | bytes 98308
  70.6 0.8 %copy-start.1 = (bf16[128,128]{1,0:T(8,128)(2,1)S(1)}, bf16[128,128]{1,0:T(8,128)(2,1)}, u32[]{:S(2)}) copy-start(bf16[128,128]{1,0:T(8,128)(2,1)} %get-tuple-element.17) | copy-start | bytes 98308
  71.4 0.8 %copy-start.4 = (bf16[96,128]{1,0:T(8,128)(2,1)S(1)}, bf16[96,128]{1,0:T(8,128)(2,1)}, u32[]{:S(2)}) copy-start(bf16[96,128]{1,0:T(8,128)(2,1)} %get-tuple-element.18) | copy-start | bytes 73732
  72.1 0.7 %copy-start.3 = (bf16[96,128]{1,0:T(8,128)(2,1)S(1)}, bf16[96,128]{1,0:T(8,128)(2,1)}, u32[]{:S(2)}) copy-start(bf16[96,128]{1,0:T(8,128)(2,1)} %get-tuple-element.19) | copy-start | bytes 73732
  72.9 0.7 copy-start.5

commit v2 on v1

v2 whole, which is shorter than its diff:
```python
import functools
import math

import jax
import jax.numpy as jnp
from jax import lax
from jax.experimental import pallas as pl
from jax.experimental.pallas import tpu as pltpu
from jax.sharding import PartitionSpec as P

EPS = 1e-06
BF = jnp.bfloat16
F32 = jnp.float32
NT = (((1,), (1,)), ((), ()))
NN = (((1,), (0,)), ((), ()))
DH = 128
TOK = 128
QH = 8
NQ = TOK * QH
Q2 = 2 * NQ
OWN = 96
GR = 4 * OWN
NG = 4
KEYS = NG * GR
QB = 256
SCALE = 1.0 / math.sqrt(DH)
C2 = SCALE / math.log(2.0)
LOW = -1e30
MESH = pl.DeviceIdType.MESH


def dot(a, b, dims):
    return lax.dot_general(a, b, dims, preferred_element_type=F32)


def rms(x):
    return lax.rsqrt(jnp.mean(x * x, axis=-1, keepdims=True) + EPS)


def norm_back(x, gain, up):
    r = rms(x)
    g = up * gain
    return r * g - x * (r * r * r * jnp.mean(x * g, axis=-1, keepdims=True))


def row_near(d):
    return ((d - 1) * 4 + 2) * OWN


def row_far(d):
    return d * 4 * OWN


ROW_FAR0 = OWN
ROW_FAR4 = (3 * 4 + 3) * OWN
HALF = OWN // 2


def kernel(
    cq_hbm, ck, cv, pk, pv, live_ref, q_gain, k_gain, dout_hbm,
    out_hbm, dq_hbm, dck_hbm, dcv_hbm, dpk_hbm, dpv_hbm, gains_hbm,
    cq, d_out, out, dq, dck, dcv, dpk, dpv, gains,
    kv, q, do, ownkv, trans, s_buf, e_buf, f_buf, dp_buf, e_own, dp_own, ok_t, dq_t, o_rem, dq_rem, m_run,
    m_at, stat, stat_rem, fac, part, y_out, y_in, y4_out, y4_in, z_out, z_in, g_buf,
    io_s, za_s, za_r, y_s, y_r, c_s, c_r, ry_s, ry_r, rz_s, rz_r, g_s, g_r,
):
    read_q = pltpu.make_async_copy(cq_hbm, cq, io_s.at[0])
    read_d = pltpu.make_async_copy(dout_hbm, d_out, io_s.at[1])
    read_q.start()
    read_d.start()

    sample = lax.axis_index("sample")
    px = lax.axis_index("prompt")
    hy = lax.axis_index("head")
    core = lax.rem(sample, 2)
    y = lax.rem(sample // 2, 2)
    z = sample // 4

    def at(z_, y_, c_):
        return z_ * 4 + y_ * 2 + c_

    sib = {"sample": at(z, y, 1 - core)}
    ynb = {"sample": at(z, 1 - y, core)}

    def z_dev(d):
        return {"sample": at(lax.rem(z + d + 8, 8), y, core)}

    my_slot = (px * 2 + core, z, hy * 2 + y)

    def partner(r, i):
        if r == 0:
            return {"prompt": i // 2, "sample": at(z, y, lax.rem(i, 2))}
        if r == 1:
            return {"sample": at(i, y, core)}
        return {"head": i // 2, "sample": at(z, lax.rem(i, 2), core)}

    def send(src, dst, ss, rs, dev):
        return pltpu.make_async_remote_copy(
            src_ref=src, dst_ref=dst, send_sem=ss, recv_sem=rs, device_id=dev, device_id_type=MESH
        )

    barrier = pltpu.get_barrier_semaphore()
    for r in (1, 2, 0):
        for k in range(1, 8):
            pl.semaphore_signal(
                barrier, inc=1, device_id=partner(r, lax.rem(my_slot[r] + k, 8)), device_id_type=MESH
            )

    kg = k_gain[...]
    qg = q_gain[...]
    pk_raw = pk[...].astype(F32)
    kv[0:OWN, 0:DH] = (pk_raw * rms(pk_raw) * kg).astype(BF)
    kv[0:OWN, DH:] = pv[...]
    pl.semaphore_wait(barrier, 21)

    def rows(start, count=OWN):
        return kv.at[pl.ds(start, count), :]

    z_plan = (
        (-1, row_near(1), 0, OWN),
        (1, row_near(1) + OWN, 0, OWN),
        (-2, row_near(2), 0, OWN),
        (2, row_near(2) + OWN, 0, OWN),
        (-1, row_near(3), row_near(2), OWN),
        (1, row_near(3) + OWN, row_near(2) + OWN, OWN),
        (-2, row_near(4), row_near(2), HALF),
        (2, row_near(4) + HALF, row_near(2) + OWN + HALF, HALF),
    )

    def copy_z(i):
        to, dst, src, count = z_plan[i]
        return send(rows(src, count), rows(dst, count), za_s.at[i], za_r.at[i], z_dev(to))

    y_plan = (
        [(ROW_FAR0, 0)]
        + [(row_far(d), row_near(d)) for d in (1, 2, 3)]
        + [(row_far(d) + OWN, row_near(d) + OWN) for d in (1, 2, 3)]
        + [(ROW_FAR4, row_near(4))]
    )

    def copy_y(i):
        dst, src = y_plan[i]
        return send(rows(src), rows(dst), y_s.at[i], y_r.at[i], ynb)

    for i in (2, 3, 0, 1):
        copy_z(i).start()
    copy_y(0).start()

    live = live_ref[0, 0]
    live_rows = lax.broadcasted_iota(jnp.int32, (TOK, 1), 0) < live
    read_q.wait()
    for h in range(QH):
        x = cq[:, h * DH : (h + 1) * DH].astype(F32)
        q[h * TOK : (h + 1) * TOK, :] = (x * rms(x) * qg).astype(BF)
    copy_q = send(q.at[0:NQ, :], q.at[NQ:, :], c_s.at[0], c_r.at[0], sib)
    copy_q.start()
    read_d.wait()
    for h in range(QH):
        g = d_out[:, h * DH : (h + 1) * DH]
        do[h * TOK : (h + 1) * TOK, :] = jnp.where(live_rows, g, jnp.zeros_like(g))
    copy_do = send(do.at[0:NQ, :], do.at[NQ:, :], c_s.at[1], c_r.at[1], sib)
    copy_do.start()

    ck_raw = ck[...].astype(F32)
    ownkv[:, 0:DH] = (ck_raw * rms(ck_raw) * kg).astype(BF)
    ownkv[:, DH:] = cv[...]

    def turn(keys, vals, count):
        trans[0:DH, 0:count] = vals.astype(F32).T.astype(BF)
        trans[DH:, 0:count] = keys.astype(F32).T.astype(BF)

    m_run[...] = jnp.full((1, Q2), LOW, F32)
    stat[...] = jnp.zeros((8, Q2), F32)
    ok_t[:, NQ:] = jnp.zeros((2 * DH, NQ), F32)
    dq_t[:, NQ:] = jnp.zeros((DH, NQ), F32)
    turn(ownkv[:, 0:DH], ownkv[:, DH:], TOK)
    u_ids = lax.broadcasted_iota(jnp.int32, (TOK, QB), 0)
    t_ids = lax.rem(lax.broadcasted_iota(jnp.int32, (TOK, QB), 1), TOK)
    allowed = u_ids <= t_ids
    for b in range(NQ // QB):
        sl = slice(b * QB, (b + 1) * QB)
        s = jnp.where(allowed, dot(ownkv[:, 0:DH], q[sl, :], NT), LOW)
        dp = dot(ownkv[:, DH:], do[sl, :], NT)
        m = jnp.max(s, axis=0, keepdims=True)
        e = jnp.exp2((s - m) * C2)
        eb = e.astype(BF)
        ed = e * dp
        e_own[:, sl] = eb
        dp_own[:, sl] = dp
        m_run[:, sl] = m
        stat[1:2, sl] = jnp.sum(e, axis=0, keepdims=True)
        stat[2:3, sl] = jnp.sum(ed, axis=0, keepdims=True)
        ok_t[:, sl] = dot(trans[:, 0:TOK], eb, NN)
        dq_t[:, sl] = dot(trans[DH:, 0:TOK], ed.astype(BF), NN)
    m_at[NG] = m_run[...]

    for i in range(4):
        copy_z(i).wait_recv()
    for i in range(4, 8):
        copy_z(i).start()
    for i in (1, 4, 2, 5):
        copy_y(i).start()
    copy_q.wait_recv()
    copy_do.wait_recv()

    def forward(g, carry):
        @pl.when(g == 0)
        def _():
            copy_y(0).wait_recv()

        @pl.when(g == 1)
        def _():
            copy_y(1).wait_recv()
            copy_y(4).wait_recv()

        @pl.when(g == 2)
        def _():
            copy_z(4).wait_recv()
            copy_z(5).wait_recv()
            copy_y(3).start()
            copy_y(6).start()
            copy_z(6).wait_recv()
            copy_z(7).wait_recv()
            copy_y(7).start()
            copy_y(2).wait_recv()
            copy_y(5).wait_recv()

        @pl.when(g == 3)
        def _():
            copy_y(3).wait_recv()
            copy_y(6).wait_recv()
            copy_y(7).wait_recv()

        at_rows = pl.ds(pl.multiple_of(g * GR, GR), GR)
        keys = kv[at_rows, 0:DH]
        vals = kv[at_rows, DH:]
        turn(keys, vals, GR)
        tiles = Q2 // QB
        mx, al, mc = {}, {}, {}

        def sl(b):
            return slice(b * QB, (b + 1) * QB)

        for t in range(tiles + 2):
            if 1 <= t <= tiles:
                b = t - 1
                m_old = m_run[:, sl(b)]
                m_new = jnp.maximum(m_old, mx[b])
                m_run[:, sl(b)] = m_new
                al[b] = jnp.exp2((m_old - m_new) * C2)
                mc[b] = m_new * C2
            if t < tiles:
                s = dot(keys, q[sl(t), :], NT)
                s_buf[:, sl(t)] = s
                mx[t] = jnp.max(s, axis=0, keepdims=True)
                dp_buf[at_rows, sl(t)] = dot(vals, do[sl(t), :], NT)
            if 1 <= t <= tiles:
                b = t - 1
                e = jnp.exp2(s_buf[:, sl(b)] * C2 - mc[b])
                ed = e * dp_buf[at_rows, sl(b)]
                e_buf[at_rows, sl(b)] = e.astype(BF)
                f_buf[:, sl(b)] = ed.astype(BF)
                stat[1:2, sl(b)] = stat[1:2, sl(b)] * al[b] + jnp.sum(e, axis=0, keepdims=True)
                stat[2:3, sl(b)] = stat[2:3, sl(b)] * al[b] + jnp.sum(ed, axis=0, keepdims=True)
            if t >= 2:
                b = t - 2
                ok_t[:, sl(b)] = ok_t[:, sl(b)] * al[b] + dot(trans[...], e_buf[at_rows, sl(b)], NN)
                dq_t[:, sl(b)] = dq_t[:, sl(b)] * al[b] + dot(trans[DH:, :], f_buf[:, sl(b)], NN)
        m_at[g] = m_run[...]
        return carry

    lax.fori_loop(0, NG, forward, 0)

    stat[0:1, :] = m_run[...]
    copy_st = send(stat, stat_rem, c_s.at[2], c_r.at[2], sib)
    copy_st.start()
    copy_st.wait_recv()
    for half in range(2):
        mine = slice(half * NQ, (half + 1) * NQ)
        other = slice((1 - half) * NQ, (2 - half) * NQ)
        m_a, m_b = stat[0:1, mine], stat_rem[0:1, other]
        m_f = jnp.maximum(m_a, m_b)
        w_a, w_b = jnp.exp2((m_a - m_f) * C2), jnp.exp2((m_b - m_f) * C2)
        inv = 1.0 / (stat[1:2, mine] * w_a + stat_rem[1:2, other] * w_b)
        for i in range(NG + (1 - half)):
            fac[i, :, mine] = jnp.exp2((m_at[i, :, mine] - m_f) * C2) * inv
        row_dot = (stat[2:3, mine] * w_a + stat_rem[2:3, other] * w_b) * inv
        fac[NG + 1, :, mine] = row_dot
        own = w_a * inv
        ok_t[0:DH, mine] = ok_t[0:DH, mine] * own
        dq_t[:, mine] = (dq_t[:, mine] - ok_t[DH:, mine] * row_dot) * own
    copy_dq = send(dq_t.at[:, NQ:], dq_rem, c_s.at[4], c_r.at[4], sib)
    copy_dq.start()
    copy_o = send(ok_t.at[0:DH, NQ:], o_rem, c_s.at[3], c_r.at[3], sib)
    copy_o.start()

    def g_start(r, value):
        g_buf[r, my_slot[r]] = value
        for k in range(1, 8):
            send(
                g_buf.at[r, my_slot[r]], g_buf.at[r, my_slot[r]], g_s.at[r, k], g_r.at[r, my_slot[r]],
                partner(r, lax.rem(my_slot[r] + k, 8)),
            ).start()

    def g_wait(r):
        for k in range(1, 8):
            j = lax.rem(my_slot[r] + k, 8)
            send(
                g_buf.at[r, j], g_buf.at[r, j], g_s.at[r, k], g_r.at[r, j], partner(r, j)
            ).wait_recv()
        total = g_buf[r, 0]
        for k in range(1, 8):
            total = total + g_buf[r, k]
        return total

    pairs = dot(dq_t[...].astype(BF), q[...], NN)
    eye = lax.broadcasted_iota(jnp.int32, (DH, DH), 0) == lax.broadcasted_iota(jnp.int32, (DH, DH), 1)
    g_start(0, jnp.sum(jnp.where(eye, pairs, 0.0).reshape(DH // 8, 8, DH), axis=0))

    def copy_ry(g):
        return send(y_out.at[g], y_in.at[g], ry_s.at[g], ry_r.at[g], ynb)

    copy_ry0 = send(y_out.at[0, OWN:, :], y_in.at[0, OWN:, :], ry_s.at[0], ry_r.at[0], ynb)
    copy_ry4 = send(y4_out, y4_in, ry_s.at[4], ry_r.at[4], ynb)

    rz_plan = (
        (1, 0, 0, OWN), (-1, 1, 0, OWN), (2, 2, 0, OWN), (-2, 3, 0, OWN),
        (1, 4, 0, OWN), (-1, 5, 0, OWN), (2, 6, 0, HALF), (-2, 6, HALF, HALF),
    )

    def copy_rz(i):
        to, slot, start, count = rz_plan[i]
        at_slot = (slot, pl.ds(start, count))
        return send(z_out.at[at_slot], z_in.at[at_slot], rz_s.at[i], rz_r.at[i], z_dev(to))

    def backward(i, carry):
        g = NG - 1 - i
        at_rows = pl.ds(pl.multiple_of(g * GR, GR), GR)
        dk = jnp.zeros((GR, DH), F32)
        dv = jnp.zeros((GR, DH), F32)
        for b in range(Q2 // QB):
            sl = slice(b * QB, (b + 1) * QB)
            p = e_buf[at_rows, sl].astype(F32) * fac[g, :, sl]
            pb = p.astype(BF)
            ds = (p * (dp_buf[at_rows, sl] - fac[NG + 1, :, sl])).astype(BF)
            dv = dv + dot(pb, do[sl, :], NN)
            dk = dk + dot(ds, q[sl, :], NN)
        part[g, :, 0:DH] = dk
        part[g, :, DH:] = dv
        y_out[g] = part[g, 0 : 2 * OWN, :].astype(BF)

        @pl.when(g > 0)
        def _():
            copy_ry(g).start()

        @pl.when(g == 0)
        def _():
            copy_ry0.start()

        @pl.when(g == 3)
        def _():
            y4_out[...] = part[3, 3 * OWN :, :].astype(BF)
            copy_ry4.start()

        @pl.when(g == 1)
        def _():
            copy_ry(3).wait_recv()
            acc = part[2, 2 * OWN :, :] + y_in[3].astype(F32)
            z_out[4] = acc[0:OWN].astype(BF)
            z_out[5] = acc[OWN:].astype(BF)
            copy_rz(4).start()
            copy_rz(5).start()
            copy_ry4.wait_recv()
            z_out[6] = (part[3, 2 * OWN : 3 * OWN, :] + y4_in[...].astype(F32)).astype(BF)
            copy_rz(6).start()
            copy_rz(7).start()

        return carry

    lax.fori_loop(0, NG, backward, 0)

    g_start(1, g_wait(0))
    copy_ry(1).wait_recv()
    acc1 = part[0, 2 * OWN :, :] + y_in[1].astype(F32)
    z_out[0] = acc1[0:OWN].astype(BF)
    z_out[1] = acc1[OWN:].astype(BF)
    copy_rz(0).start()
    copy_rz(1).start()

    dk = jnp.zeros((TOK, DH), F32)
    dv = jnp.zeros((TOK, DH), F32)
    for b in range(NQ // QB):
        sl = slice(b * QB, (b + 1) * QB)
        p = e_own[:, sl].astype(F32) * fac[NG, :, sl]
        pb = p.astype(BF)
        ds = (p * (dp_own[:, sl] - fac[NG + 1, :, sl])).astype(BF)
        dv = dv + dot(pb, do[sl, :], NN)
        dk = dk + dot(ds, q[sl, :], NN)
    dck[...] = norm_back(ck_raw, kg, dk * SCALE).astype(BF)
    dcv[...] = dv.astype(BF)
    writes = [
        pltpu.make_async_copy(dck, dck_hbm, io_s.at[2]),
        pltpu.make_async_copy(dcv, dcv_hbm, io_s.at[3]),
    ]
    for w in writes:
        w.start()

    copy_o.wait_recv()
    for h in range(QH):
        sl = slice(h * TOK, (h + 1) * TOK)
        x = (ok_t[0:DH, sl] + o_rem[:, sl]).T
        out[:, h * DH : (h + 1) * DH] = jnp.where(live_rows, x, 0.0).astype(BF)
    write_o = pltpu.make_async_copy(out, out_hbm, io_s.at[4])
    write_o.start()

    g_start(2, g_wait(1))
    copy_ry(2).wait_recv()
    for i in range(4, 8):
        copy_rz(i).wait_recv()
    acc2 = part[1, 2 * OWN :, :] + y_in[2].astype(F32)
    far = z_in[6].astype(F32)
    up2 = acc2[0:OWN] + z_in[4].astype(F32)
    down2 = acc2[OWN:] + z_in[5].astype(F32)
    z_out[2, 0:HALF, :] = (up2[0:HALF] + far[0:HALF]).astype(BF)
    z_out[2, HALF:, :] = up2[HALF:].astype(BF)
    z_out[3, 0:HALF, :] = down2[0:HALF].astype(BF)
    z_out[3, HALF:, :] = (down2[HALF:] + far[HALF:]).astype(BF)
    copy_rz(2).start()
    copy_rz(3).start()

    copy_dq.wait_recv()
    for h in range(QH):
        sl = slice(h * TOK, (h + 1) * TOK)
        up = (dq_t[:, sl] + dq_rem[:, sl]).T * SCALE
        x = cq[:, h * DH : (h + 1) * DH].astype(F32)
        dq[:, h * DH : (h + 1) * DH] = norm_back(x, qg, up).astype(BF)
    write_dq = pltpu.make_async_copy(dq, dq_hbm, io_s.at[5])
    write_dq.start()

    copy_ry0.wait_recv()
    for i in range(4):
        copy_rz(i).wait_recv()
    total = part[0, 0:OWN, :] + y_in[0, OWN:, :].astype(F32)
    for i in range(4):
        total = total + z_in[i].astype(F32)
    dpk[...] = norm_back(pk_raw, kg, total[:, 0:DH] * SCALE).astype(BF)
    dpv[...] = total[:, DH:].astype(BF)
    write_pk = pltpu.make_async_copy(dpk, dpk_hbm, io_s.at[6])
    write_pv = pltpu.make_async_copy(dpv, dpv_hbm, io_s.at[7])
    write_pk.start()
    write_pv.start()

    g_sum = jnp.sum(g_wait(2), axis=0, keepdims=True) * (SCALE / math.sqrt(GAIN_ROWS))
    gains[0:1, :] = g_sum / qg
    gains[1:2, :] = g_sum / kg
    write_g = pltpu.make_async_copy(gains, gains_hbm, io_s.at[8])
    write_g.start()

    for i in range(8):
        copy_z(i).wait_send()
        copy_y(i).wait_send()
        copy_rz(i).wait_send()
    for c in (copy_q, copy_do, copy_st, copy_o, copy_dq, copy_ry0, copy_ry4):
        c.wait_send()
    for g in range(1, NG):
        copy_ry(g).wait_send()
    for r in range(3):
        for k in range(1, 8):
            j = lax.rem(my_slot[r] + k, 8)
            send(
                g_buf.at[r, my_slot[r]], g_buf.at[r, my_slot[r]], g_s.at[r, k], g_r.at[r, j], partner(r, j)
            ).wait_send()
    for w in writes + [write_o, write_dq, write_pk, write_pv, write_g]:
        w.wait()


def place(*refs):
    count = (len(refs) - 1) // 3
    src, dst, held, sems = refs[:count], refs[count : 2 * count], refs[2 * count : 3 * count], refs[-1]
    reads = [pltpu.make_async_copy(src[i], held[i], sems.at[0, i]) for i in range(count)]
    writes = [pltpu.make_async_copy(held[i], dst[i], sems.at[1, i]) for i in range(count)]
    for r in reads:
        r.start()
    for r, w in zip(reads, writes):
        r.wait()
        w.start()
    for w in writes:
        w.wait()


GAIN_ROWS = 524288


def per_device(comp_q, comp_k, comp_v, prompt_k, prompt_v, lengths, q_gain, k_gain, d_out):
    vmem = pl.BlockSpec(memory_space=pltpu.VMEM)
    smem = pl.BlockSpec(memory_space=pltpu.SMEM)
    dma = pltpu.SemaphoreType.DMA
    width = QH * DH
    shapes = [
        jax.ShapeDtypeStruct((TOK, width), BF),
        jax.ShapeDtypeStruct((TOK, width), BF),
        jax.ShapeDtypeStruct((TOK, DH), BF),
        jax.ShapeDtypeStruct((TOK, DH), BF),
        jax.ShapeDtypeStruct((OWN, DH), BF),
        jax.ShapeDtypeStruct((OWN, DH), BF),
        jax.ShapeDtypeStruct((2, DH), F32),
    ]
    scratch = [
        pltpu.VMEM((TOK, width), BF),
        pltpu.VMEM((TOK, width), BF),
        pltpu.VMEM((TOK, width), BF),
        pltpu.VMEM((TOK, width), BF),
        pltpu.VMEM((TOK, DH), BF),
        pltpu.VMEM((TOK, DH), BF),
        pltpu.VMEM((OWN, DH), BF),
        pltpu.VMEM((OWN, DH), BF),
        pltpu.VMEM((2, DH), F32),
        pltpu.VMEM((KEYS, 2 * DH), BF),
        pltpu.VMEM((Q2, DH), BF),
        pltpu.VMEM((Q2, DH), BF),
        pltpu.VMEM((TOK, 2 * DH), BF),
        pltpu.VMEM((2 * DH, GR), BF),
        pltpu.VMEM((GR, Q2), F32),
        pltpu.VMEM((KEYS, Q2), BF),
        pltpu.VMEM((GR, Q2), BF),
        pltpu.VMEM((KEYS, Q2), F32),
        pltpu.VMEM((TOK, NQ), BF),
        pltpu.VMEM((TOK, NQ), F32),
        pltpu.VMEM((2 * DH, Q2), F32),
        pltpu.VMEM((DH, Q2), F32),
        pltpu.VMEM((DH, NQ), F32),
        pltpu.VMEM((DH, NQ), F32),
        pltpu.VMEM((1, Q2), F32),
        pltpu.VMEM((NG + 1, 1, Q2), F32),
        pltpu.VMEM((8, Q2), F32),
        pltpu.VMEM((8, Q2), F32),
        pltpu.VMEM((NG + 2, 1, Q2), F32),
        pltpu.VMEM((NG, GR, 2 * DH), F32),
        pltpu.VMEM((NG, 2 * OWN, 2 * DH), BF),
        pltpu.VMEM((NG, 2 * OWN, 2 * DH), BF),
        pltpu.VMEM((OWN, 2 * DH), BF),
        pltpu.VMEM((OWN, 2 * DH), BF),
        pltpu.VMEM((7, OWN, 2 * DH), BF),
        pltpu.VMEM((7, OWN, 2 * DH), BF),
        pltpu.VMEM((3, 8, 8, DH), F32),
        dma((9,)), dma((8,)), dma((8,)), dma((8,)), dma((8,)), dma((5,)), dma((5,)),
        dma((5,)), dma((5,)), dma((8,)), dma((8,)), dma((3, 8)), dma((3, 8)),
    ]
    anywhere = pl.BlockSpec(memory_space=pl.ANY)
    res = pl.pallas_call(
        kernel,
        out_shape=shapes,
        in_specs=[anywhere] + [vmem] * 4 + [smem] + [vmem] * 2 + [anywhere],
        out_specs=[anywhere] * 7,
        scratch_shapes=scratch,
        compiler_params=pltpu.CompilerParams(
            collective_id=0, has_side_effects=True, vmem_limit_bytes=56 * 2**20
        ),
    )(
        comp_q.reshape(TOK, width),
        comp_k.reshape(TOK, DH),
        comp_v.reshape(TOK, DH),
        prompt_k.reshape(OWN, DH),
        prompt_v.reshape(OWN, DH),
        lengths,
        q_gain.reshape(1, DH),
        k_gain.reshape(1, DH),
        d_out.reshape(TOK, width),
    )
    res = pl.pallas_call(
        place,
        out_shape=shapes,
        in_specs=[anywhere] * 7,
        out_specs=[anywhere] * 7,
        scratch_shapes=[pltpu.VMEM(x.shape, x.dtype) for x in shapes] + [dma((2, 7))],
    )(*res)
    return (
        res[0].reshape(1, 1, TOK, width),
        res[1].reshape(1, 1, TOK, width),
        res[2].reshape(1, 1, TOK, DH),
        res[3].reshape(1, 1, TOK, DH),
        res[4].reshape(1, OWN, DH),
        res[5].reshape(1, OWN, DH),
        res[6],
    )


def solution(mesh):
    return jax.shard_map(
        per_device,
        mesh=mesh,
        in_specs=(
            P("prompt", "sample", None, "head"),
            P("prompt", "sample", None, "head"),
            P("prompt", "sample", None, "head"),
            P("prompt", "sample", "head"),
            P("prompt", "sample", "head"),
            P("prompt", "sample"),
            P(),
            P(),
            P("prompt", "sample", None, "head"),
        ),
        out_specs=(
            P("prompt", "sample", None, "head"),
            P("prompt", "sample", None, "head"),
            P("prompt", "sample", None, "head"),
            P("prompt", "sample", None, "head"),
            P("prompt", "sample", "head"),
            P("prompt", "sample", "head"),
            P(),
        ),
        check_vma=False,
    )
```

time: 74.6 us -> 56.6 us (0.76)
  Pallas kernels: 66.8 us -> 55.1 us
  local copies, waits for them, and re-layouts: 5.97 us -> 0 us
    pallas_call x1 -> x2, Pallas kernels: 66.8 us -> 55.1 us  [the longest x1 53.2 us: per_device(): pl.pallas_call(kernel, out_shape=shapes, in_specs=[anywhere] + [vmem] * 4...]
    unnamed x19 -> x0, local copies, waits for them, and re-layouts: 5.97 us -> none
where the time goes in v2:
time: 56.6 us; the launch traced here: 56.3 us
  Pallas kernels  55.1 us (97%)
  between operations  1.29 us (2%)
    pallas_call x1, Pallas kernels, per_device(): pl.pallas_call(kernel, out_shape=shapes, in_specs=[anywhere] + [vmem] * 4...  53.2 us
    pallas_call x1, Pallas kernels, per_device(): pl.pallas_call(place, out_shape=shapes, in_specs=[anywhere] * 7, out_spec...  1.89 us

profile of v2, /device:TPU:1, one launch (start us, length us, event | category | flops | bytes accessed | tf_op | source)
XLA Modules:
  0.0 56.3 jit_solution(5087768557821091661)
XLA Ops:
  1.3 53.2 %shard_map.144 = (bf16[128,1024]{1,0:T(8,128)(2,1)}, bf16[128,1024]{1,0:T(8,128)(2,1)}, bf16[128,128]{1,0:T(8,128)(2,1)}, bf16[128,128]{1,0:T(8,128)(2,1)}, bf16...) custom-call(bf16[128,1024]{1,0:T(8,128)(2,1)} %bitcast.14, bf16[128,128]{1,0:T(8,128)(2,1)} %bitcast.16, ...), custom_call_target="tpu_custom_call" | custom-call | tf_op jit(solution)/shard_map/pallas_call | solution.py:550
  54.5 1.9 %shard_map.145 = (bf16[128,1024]{1,0:T(8,128)(2,1)}, bf16[128,1024]{1,0:T(8,128)(2,1)}, bf16[128,128]{1,0:T(8,128)(2,1)}, bf16[128,128]{1,0:T(8,128)(2,1)}, bf16...) custom-call(bf16[128,1024]{1,0:T(8,128)(2,1)} %get-tuple-element.21.refs_0_, ...), custom_call_target="tpu_custom_call" | custom-call | tf_op jit(solution)/shard_map/pallas_call | solution.py:570

commit v3 on v2

--- a/solution.py
+++ b/solution.py
@@ -48,7 +48,7 @@
 
 
 def row_far(d):
-    return d * 4 * OWN
+    return (8, 4, 12)[d - 1] * OWN
 
 
 ROW_FAR0 = OWN
@@ -61,7 +61,7 @@
     out_hbm, dq_hbm, dck_hbm, dcv_hbm, dpk_hbm, dpv_hbm, gains_hbm,
     cq, d_out, out, dq, dck, dcv, dpk, dpv, gains,
     kv, q, do, ownkv, trans, s_buf, e_buf, f_buf, dp_buf, e_own, dp_own, ok_t, dq_t, o_rem, dq_rem, m_run,
-    m_at, stat, stat_rem, fac, part, y_out, y_in, y4_out, y4_in, z_out, z_in, g_buf,
+    m_at, stat, stat_rem, fac, part, y_out, y_in, z_out, z_in, g_buf,
     io_s, za_s, za_r, y_s, y_r, c_s, c_r, ry_s, ry_r, rz_s, rz_r, g_s, g_r,
 ):
     read_q = pltpu.make_async_copy(cq_hbm, cq, io_s.at[0])
@@ -116,38 +116,48 @@
     def rows(start, count=OWN):
         return kv.at[pl.ds(start, count), :]
 
+    def halves(to, dst, src):
+        return [(to, dst, src), (to, dst + HALF, src + HALF)]
+
     z_plan = (
-        (-1, row_near(1), 0, OWN),
-        (1, row_near(1) + OWN, 0, OWN),
-        (-2, row_near(2), 0, OWN),
-        (2, row_near(2) + OWN, 0, OWN),
-        (-1, row_near(3), row_near(2), OWN),
-        (1, row_near(3) + OWN, row_near(2) + OWN, OWN),
-        (-2, row_near(4), row_near(2), HALF),
-        (2, row_near(4) + HALF, row_near(2) + OWN + HALF, HALF),
+        halves(-1, row_near(1), 0)
+        + halves(1, row_near(1) + OWN, 0)
+        + halves(-2, row_near(2), 0)
+        + halves(2, row_near(2) + OWN, 0)
+        + halves(-1, row_near(3), row_near(2))
+        + halves(1, row_near(3) + OWN, row_near(2) + OWN)
+        + [(-2, row_near(4), row_near(2)), (2, row_near(4) + HALF, row_near(2) + OWN + HALF)]
+        + halves(-2, row_far(2), ROW_FAR0)
+        + halves(2, row_far(2) + OWN, ROW_FAR0)
+        + halves(-1, row_far(3), row_far(2))
+        + halves(1, row_far(3) + OWN, row_far(2) + OWN)
+        + [(-2, ROW_FAR4, row_far(2)), (2, ROW_FAR4 + HALF, row_far(2) + OWN + HALF)]
     )
 
     def copy_z(i):
-        to, dst, src, count = z_plan[i]
-        return send(rows(src, count), rows(dst, count), za_s.at[i], za_r.at[i], z_dev(to))
-
-    y_plan = (
-        [(ROW_FAR0, 0)]
-        + [(row_far(d), row_near(d)) for d in (1, 2, 3)]
-        + [(row_far(d) + OWN, row_near(d) + OWN) for d in (1, 2, 3)]
-        + [(ROW_FAR4, row_near(4))]
-    )
+        to, dst, src = z_plan[i]
+        return send(rows(src, HALF), rows(dst, HALF), za_s.at[i], za_r.at[i], z_dev(to))
+
+    y_plan = [
+        (dst + h, src + h)
+        for dst, src in (
+            (ROW_FAR0, 0),
+            (row_far(1), row_near(1)),
+            (row_far(1) + OWN, row_near(1) + OWN),
+        )
+        for h in (0, HALF)
+    ]
 
     def copy_y(i):
         dst, src = y_plan[i]
-        return send(rows(src), rows(dst), y_s.at[i], y_r.at[i], ynb)
-
-    for i in (2, 3, 0, 1):
+        return send(rows(src, HALF), rows(dst, HALF), y_s.at[i], y_r.at[i], ynb)
+
+    for i in (4, 6, 5, 7, 0, 2, 1, 3):
         copy_z(i).start()
     copy_y(0).start()
-
-    live = live_ref[0, 0]
-    live_rows = lax.broadcasted_iota(jnp.int32, (TOK, 1), 0) < live
+    copy_y(1).start()
+
+    live_rows = lax.broadcasted_iota(jnp.int32, (TOK, 1), 0) < live_ref[...]
     read_q.wait()
     for h in range(QH):
         x = cq[:, h * DH : (h + 1) * DH].astype(F32)
@@ -194,86 +204,110 @@
         dq_t[:, sl] = dot(trans[DH:, 0:TOK], ed.astype(BF), NN)
     m_at[NG] = m_run[...]
 
-    for i in range(4):
-        copy_z(i).wait_recv()
-    for i in range(4, 8):
-        copy_z(i).start()
-    for i in (1, 4, 2, 5):
-        copy_y(i).start()
+    for h in range(2):
+        copy_y(h).wait_recv()
+        copy_z(14 + h).start()
+        copy_z(16 + h).start()
+    for h in range(2):
+        copy_z(4 + h).wait_recv()
+        copy_z(6 + h).wait_recv()
+        for i in (8 + h, 12 + h, 10 + h):
+            copy_z(i).start()
+    for h in range(2):
+        copy_z(h).wait_recv()
+        copy_z(2 + h).wait_recv()
+        copy_y(2 + h).start()
+        copy_y(4 + h).start()
     copy_q.wait_recv()
     copy_do.wait_recv()
 
+    tiles = Q2 // QB
+
+    def tile(b):
+        return slice(b * QB, (b + 1) * QB)
+
+    def rise(b, mx):
+        m_old = m_run[:, tile(b)]
+        m_new = jnp.maximum(m_old, mx)
+        m_run[:, tile(b)] = m_new
+        return jnp.exp2((m_old - m_new) * C2), m_new * C2
+
+    def scores(b, at_rows, keys, vals):
+        s = dot(keys, q[tile(b), :], NT)
+        s_buf[:, tile(b)] = s
+        dp_buf[at_rows, tile(b)] = dot(vals, do[tile(b), :], NT)
+        return jnp.max(s, axis=0, keepdims=True)
+
+    def weigh(b, at_rows, al, mc):
+        sl = tile(b)
+        e = jnp.exp2(s_buf[:, sl] * C2 - mc)
+        ed = e * dp_buf[at_rows, sl]
+        e_buf[at_rows, sl] = e.astype(BF)
+        f_buf[:, sl] = ed.astype(BF)
+        stat[1:2, sl] = stat[1:2, sl] * al + jnp.sum(e, axis=0, keepdims=True)
+        stat[2:3, sl] = stat[2:3, sl] * al + jnp.sum(ed, axis=0, keepdims=True)
+
+    def mix(b, at_rows, al):
+        sl = tile(b)
+        ok_t[:, sl] = ok_t[:, sl] * al + dot(trans[...], e_buf[at_rows, sl], NN)
+        dq_t[:, sl] = dq_t[:, sl] * al + dot(trans[DH:, :], f_buf[:, sl], NN)
+
     def forward(g, carry):
-        @pl.when(g == 0)
-        def _():
-            copy_y(0).wait_recv()
-
         @pl.when(g == 1)
         def _():
-            copy_y(1).wait_recv()
-            copy_y(4).wait_recv()
+            for h in range(2):
+                copy_z(14 + h).wait_recv()
+                copy_z(16 + h).wait_recv()
+                for j in (18 + h, 20 + h, 22 + h):
+                    copy_z(j).start()
 
         @pl.when(g == 2)
         def _():
-            copy_z(4).wait_recv()
-            copy_z(5).wait_recv()
-            copy_y(3).start()
-            copy_y(6).start()
-            copy_z(6).wait_recv()
-            copy_z(7).wait_recv()
-            copy_y(7).start()
-            copy_y(2).wait_recv()
-            copy_y(5).wait_recv()
-
-        @pl.when(g == 3)
-        def _():
-            copy_y(3).wait_recv()
-            copy_y(6).wait_recv()
-            copy_y(7).wait_recv()
+            for i in range(2, 6):
+                copy_y(i).wait_recv()
+            for i in range(8, 12):
+                copy_z(i).wait_recv()
 
         at_rows = pl.ds(pl.multiple_of(g * GR, GR), GR)
         keys = kv[at_rows, 0:DH]
         vals = kv[at_rows, DH:]
         turn(keys, vals, GR)
-        tiles = Q2 // QB
         mx, al, mc = {}, {}, {}
-
-        def sl(b):
-            return slice(b * QB, (b + 1) * QB)
-
         for t in range(tiles + 2):
             if 1 <= t <= tiles:
-                b = t - 1
-                m_old = m_run[:, sl(b)]
-                m_new = jnp.maximum(m_old, mx[b])
-                m_run[:, sl(b)] = m_new
-                al[b] = jnp.exp2((m_old - m_new) * C2)
-                mc[b] = m_new * C2
+                al[t - 1], mc[t - 1] = rise(t - 1, mx[t - 1])
             if t < tiles:
-                s = dot(keys, q[sl(t), :], NT)
-                s_buf[:, sl(t)] = s
-                mx[t] = jnp.max(s, axis=0, keepdims=True)
-                dp_buf[at_rows, sl(t)] = dot(vals, do[sl(t), :], NT)
+                mx[t] = scores(t, at_rows, keys, vals)
             if 1 <= t <= tiles:
-                b = t - 1
-                e = jnp.exp2(s_buf[:, sl(b)] * C2 - mc[b])
-                ed = e * dp_buf[at_rows, sl(b)]
-                e_buf[at_rows, sl(b)] = e.astype(BF)
-                f_buf[:, sl(b)] = ed.astype(BF)
-                stat[1:2, sl(b)] = stat[1:2, sl(b)] * al[b] + jnp.sum(e, axis=0, keepdims=True)
-                stat[2:3, sl(b)] = stat[2:3, sl(b)] * al[b] + jnp.sum(ed, axis=0, keepdims=True)
+                weigh(t - 1, at_rows, al[t - 1], mc[t - 1])
             if t >= 2:
-                b = t - 2
-                ok_t[:, sl(b)] = ok_t[:, sl(b)] * al[b] + dot(trans[...], e_buf[at_rows, sl(b)], NN)
-                dq_t[:, sl(b)] = dq_t[:, sl(b)] * al[b] + dot(trans[DH:, :], f_buf[:, sl(b)], NN)
+                mix(t - 2, at_rows, al[t - 2])
         m_at[g] = m_run[...]
         return carry
 
-    lax.fori_loop(0, NG, forward, 0)
+    lax.fori_loop(0, NG - 1, forward, 0)
+
+    for i in (12, 13, 18, 19, 20, 21, 22, 23):
+        copy_z(i).wait_recv()
+    last = slice((NG - 1) * GR, NG * GR)
+    keys = kv[last, 0:DH]
+    vals = kv[last, DH:]
+    mx, al, mc = {}, {}, {}
+    for t in range(tiles + 1):
+        if t >= 1:
+            al[t - 1], mc[t - 1] = rise(t - 1, mx[t - 1])
+        if t < tiles:
+            mx[t] = scores(t, last, keys, vals)
+        if t >= 1:
+            weigh(t - 1, last, al[t - 1], mc[t - 1])
+    m_at[NG - 1] = m_run[...]
 
     stat[0:1, :] = m_run[...]
     copy_st = send(stat, stat_rem, c_s.at[2], c_r.at[2], sib)
     copy_st.start()
+    turn(keys, vals, GR)
+    for b in range(tiles):
+        mix(b, last, al[b])
     copy_st.wait_recv()
     for half in range(2):
         mine = slice(half * NQ, (half + 1) * NQ)
@@ -284,15 +318,8 @@
         inv = 1.0 / (stat[1:2, mine] * w_a + stat_rem[1:2, other] * w_b)
         for i in range(NG + (1 - half)):
             fac[i, :, mine] = jnp.exp2((m_at[i, :, mine] - m_f) * C2) * inv
-        row_dot = (stat[2:3, mine] * w_a + stat_rem[2:3, other] * w_b) * inv
-        fac[NG + 1, :, mine] = row_dot
-        own = w_a * inv
-        ok_t[0:DH, mine] = ok_t[0:DH, mine] * own
-        dq_t[:, mine] = (dq_t[:, mine] - ok_t[DH:, mine] * row_dot) * own
-    copy_dq = send(dq_t.at[:, NQ:], dq_rem, c_s.at[4], c_r.at[4], sib)
-    copy_dq.start()
-    copy_o = send(ok_t.at[0:DH, NQ:], o_rem, c_s.at[3], c_r.at[3], sib)
-    copy_o.start()
+        fac[NG + 1, :, mine] = (stat[2:3, mine] * w_a + stat_rem[2:3, other] * w_b) * inv
+        fac[NG + 2, :, mine] = w_a * inv
 
     def g_start(r, value):
         g_buf[r, my_slot[r]] = value
@@ -313,33 +340,41 @@
             total = total + g_buf[r, k]
         return total
 
-    pairs = dot(dq_t[...].astype(BF), q[...], NN)
-    eye = lax.broadcasted_iota(jnp.int32, (DH, DH), 0) == lax.broadcasted_iota(jnp.int32, (DH, DH), 1)
-    g_start(0, jnp.sum(jnp.where(eye, pairs, 0.0).reshape(DH // 8, 8, DH), axis=0))
-
-    def copy_ry(g):
-        return send(y_out.at[g], y_in.at[g], ry_s.at[g], ry_r.at[g], ynb)
-
-    copy_ry0 = send(y_out.at[0, OWN:, :], y_in.at[0, OWN:, :], ry_s.at[0], ry_r.at[0], ynb)
-    copy_ry4 = send(y4_out, y4_in, ry_s.at[4], ry_r.at[4], ynb)
-
-    rz_plan = (
-        (1, 0, 0, OWN), (-1, 1, 0, OWN), (2, 2, 0, OWN), (-2, 3, 0, OWN),
-        (1, 4, 0, OWN), (-1, 5, 0, OWN), (2, 6, 0, HALF), (-2, 6, HALF, HALF),
-    )
+    def copy_ry(g, h):
+        at_rows = pl.ds(h * HALF, HALF)
+        return [
+            send(
+                y_out.at[g, sign, at_rows], y_in.at[g, sign, at_rows],
+                ry_s.at[g, sign, h], ry_r.at[g, sign, h], ynb,
+            )
+            for sign in range(2)
+        ]
+
+    def copy_ry4(h):
+        at_rows = pl.ds(h * HALF, HALF)
+        return send(
+            y_out.at[1, 0, at_rows], y_in.at[1, 0, at_rows], ry_s.at[1, 0, h], ry_r.at[1, 0, h], ynb
+        )
+
+    copy_ry0 = send(y_out.at[0, 0], y_in.at[0, 0], ry_s.at[0, 0, 0], ry_r.at[0, 0, 0], ynb)
+
+    rz_plan = [
+        (to, slot, h)
+        for slot, to in ((0, 1), (1, -1), (2, 2), (3, -2), (4, 1), (5, -1))
+        for h in (0, HALF)
+    ] + [(2, 6, 0), (-2, 6, HALF)]
+    rz_plan += [(to, slot, h) for slot, to in ((7, 1), (8, -1)) for h in (0, HALF)]
 
     def copy_rz(i):
-        to, slot, start, count = rz_plan[i]
-        at_slot = (slot, pl.ds(start, count))
+        to, slot, h = rz_plan[i]
+        at_slot = (slot, pl.ds(h, HALF))
         return send(z_out.at[at_slot], z_in.at[at_slot], rz_s.at[i], rz_r.at[i], z_dev(to))
 
-    def backward(i, carry):
-        g = NG - 1 - i
-        at_rows = pl.ds(pl.multiple_of(g * GR, GR), GR)
+    def gradients(g, at_rows):
         dk = jnp.zeros((GR, DH), F32)
         dv = jnp.zeros((GR, DH), F32)
-        for b in range(Q2 // QB):
-            sl = slice(b * QB, (b + 1) * QB)
+        for b in range(tiles):
+            sl = tile(b)
             p = e_buf[at_rows, sl].astype(F32) * fac[g, :, sl]
             pb = p.astype(BF)
             ds = (p * (dp_buf[at_rows, sl] - fac[NG + 1, :, sl])).astype(BF)
@@ -347,45 +382,72 @@
             dk = dk + dot(ds, q[sl, :], NN)
         part[g, :, 0:DH] = dk
         part[g, :, DH:] = dv
-        y_out[g] = part[g, 0 : 2 * OWN, :].astype(BF)
-
-        @pl.when(g > 0)
+
+    gradients(NG - 1, last)
+    y_out[3, 0] = part[3, 0:OWN, :].astype(BF)
+    y_out[3, 1] = part[3, OWN : 2 * OWN, :].astype(BF)
+    y_out[1, 0] = part[3, 3 * OWN :, :].astype(BF)
+    for h in range(2):
+        for c in copy_ry(3, h):
+            c.start()
+        copy_ry4(h).start()
+
+    own = fac[NG + 2]
+    ok_t[0:DH, :] = ok_t[0:DH, :] * own
+    dq_t[...] = (dq_t[...] - ok_t[DH:, :] * fac[NG + 1]) * own
+    copy_dq = send(dq_t.at[:, NQ:], dq_rem, c_s.at[4], c_r.at[4], sib)
+    copy_dq.start()
+    copy_o = send(ok_t.at[0:DH, NQ:], o_rem, c_s.at[3], c_r.at[3], sib)
+    copy_o.start()
+    pairs = dot(dq_t[...].astype(BF), q[...], NN)
+    eye = lax.broadcasted_iota(jnp.int32, (DH, DH), 0) == lax.broadcasted_iota(jnp.int32, (DH, DH), 1)
+    g_start(0, jnp.sum(jnp.where(eye, pairs, 0.0).reshape(DH // 8, 8, DH), axis=0))
+
+    def far_sums(h):
+        for c in copy_ry(3, h):
+            c.wait_recv()
+        copy_ry4(h).wait_recv()
+        r = slice(h * HALF, (h + 1) * HALF)
+        for sign in range(2):
+            start = (2 + sign) * OWN + h * HALF
+            z_out[4 + sign, r, :] = (
+                part[2, start : start + HALF, :] + y_in[3, sign, r, :].astype(F32)
+            ).astype(BF)
+            copy_rz(8 + 2 * sign + h).start()
+        start = 2 * OWN + h * HALF
+        z_out[6, r, :] = (part[3, start : start + HALF, :] + y_in[1, 0, r, :].astype(F32)).astype(BF)
+        copy_rz(12 + h).start()
+
+    def backward(i, carry):
+        g = NG - 2 - i
+        gradients(g, pl.ds(pl.multiple_of(g * GR, GR), GR))
+
+        @pl.when(g == 2)
         def _():
-            copy_ry(g).start()
-
-        @pl.when(g == 0)
-        def _():
-            copy_ry0.start()
-
-        @pl.when(g == 3)
-        def _():
-            y4_out[...] = part[3, 3 * OWN :, :].astype(BF)
-            copy_ry4.start()
+            z_out[7] = part[2, 0:OWN, :].astype(BF)
+            z_out[8] = part[2, OWN : 2 * OWN, :].astype(BF)
+            for j in range(14, 18):
+                copy_rz(j).start()
 
         @pl.when(g == 1)
         def _():
-            copy_ry(3).wait_recv()
-            acc = part[2, 2 * OWN :, :] + y_in[3].astype(F32)
-            z_out[4] = acc[0:OWN].astype(BF)
-            z_out[5] = acc[OWN:].astype(BF)
-            copy_rz(4).start()
-            copy_rz(5).start()
-            copy_ry4.wait_recv()
-            z_out[6] = (part[3, 2 * OWN : 3 * OWN, :] + y4_in[...].astype(F32)).astype(BF)
-            copy_rz(6).start()
-            copy_rz(7).start()
+            y_out[2, 0] = part[1, 0:OWN, :].astype(BF)
+            y_out[2, 1] = part[1, OWN : 2 * OWN, :].astype(BF)
+            for h in range(2):
+                for c in copy_ry(2, h):
+                    c.start()
+            far_sums(0)
 
         return carry
 
-    lax.fori_loop(0, NG, backward, 0)
-
+    lax.fori_loop(0, NG - 1, backward, 0)
+
+    far_sums(1)
+    z_out[0] = part[0, 2 * OWN : 3 * OWN, :].astype(BF)
+    z_out[1] = part[0, 3 * OWN :, :].astype(BF)
+    for j in range(4):
+        copy_rz(j).start()
     g_start(1, g_wait(0))
-    copy_ry(1).wait_recv()
-    acc1 = part[0, 2 * OWN :, :] + y_in[1].astype(F32)
-    z_out[0] = acc1[0:OWN].astype(BF)
-    z_out[1] = acc1[OWN:].astype(BF)
-    copy_rz(0).start()
-    copy_rz(1).start()
 
     dk = jnp.zeros((TOK, DH), F32)
     dv = jnp.zeros((TOK, DH), F32)
@@ -414,19 +476,27 @@
     write_o.start()
 
     g_start(2, g_wait(1))
-    copy_ry(2).wait_recv()
-    for i in range(4, 8):
-        copy_rz(i).wait_recv()
-    acc2 = part[1, 2 * OWN :, :] + y_in[2].astype(F32)
-    far = z_in[6].astype(F32)
-    up2 = acc2[0:OWN] + z_in[4].astype(F32)
-    down2 = acc2[OWN:] + z_in[5].astype(F32)
-    z_out[2, 0:HALF, :] = (up2[0:HALF] + far[0:HALF]).astype(BF)
-    z_out[2, HALF:, :] = up2[HALF:].astype(BF)
-    z_out[3, 0:HALF, :] = down2[0:HALF].astype(BF)
-    z_out[3, HALF:, :] = (down2[HALF:] + far[HALF:]).astype(BF)
-    copy_rz(2).start()
-    copy_rz(3).start()
+    for j in range(14, 18):
+        copy_rz(j).wait_recv()
+    y_out[0, 0] = (
+        part[0, OWN : 2 * OWN, :] + z_in[7].astype(F32) + z_in[8].astype(F32)
+    ).astype(BF)
+    copy_ry0.start()
+    for h in range(2):
+        for c in copy_ry(2, h):
+            c.wait_recv()
+        copy_rz(8 + h).wait_recv()
+        copy_rz(10 + h).wait_recv()
+        copy_rz(12 + h).wait_recv()
+        r = slice(h * HALF, (h + 1) * HALF)
+        for sign in range(2):
+            start = (2 + sign) * OWN + h * HALF
+            acc = part[1, start : start + HALF, :] + y_in[2, sign, r, :].astype(F32)
+            acc = acc + z_in[4 + sign, r, :].astype(F32)
+            if sign == h:
+                acc = acc + z_in[6, r, :].astype(F32)
+            z_out[2 + sign, r, :] = acc.astype(BF)
+            copy_rz(4 + 2 * sign + h).start()
 
     copy_dq.wait_recv()
     for h in range(QH):
@@ -438,9 +508,9 @@
     write_dq.start()
 
     copy_ry0.wait_recv()
-    for i in range(4):
-        copy_rz(i).wait_recv()
-    total = part[0, 0:OWN, :] + y_in[0, OWN:, :].astype(F32)
+    for j in range(8):
+        copy_rz(j).wait_recv()
+    total = part[0, 0:OWN, :] + y_in[0, 0].astype(F32)
     for i in range(4):
         total = total + z_in[i].astype(F32)
     dpk[...] = norm_back(pk_raw, kg, total[:, 0:DH] * SCALE).astype(BF)
@@ -456,14 +526,18 @@
     write_g = pltpu.make_async_copy(gains, gains_hbm, io_s.at[8])
     write_g.start()
 
-    for i in range(8):
+    for i in range(24):
         copy_z(i).wait_send()
+    for i in range(18):
+        copy_rz(i).wait_send()
+    for i in range(6):
         copy_y(i).wait_send()
-        copy_rz(i).wait_send()
-    for c in (copy_q, copy_do, copy_st, copy_o, copy_dq, copy_ry0, copy_ry4):
+    for c in (copy_q, copy_do, copy_st, copy_o, copy_dq, copy_ry0):
         c.wait_send()
-    for g in range(1, NG):
-        copy_ry(g).wait_send()
+    for h in range(2):
+        copy_ry4(h).wait_send()
+        for c in copy_ry(2, h) + copy_ry(3, h):
+            c.wait_send()
     for r in range(3):
         for k in range(1, 8):
             j = lax.rem(my_slot[r] + k, 8)
@@ -493,7 +567,6 @@
 
 def per_device(comp_q, comp_k, comp_v, prompt_k, prompt_v, lengths, q_gain, k_gain, d_out):
     vmem = pl.BlockSpec(memory_space=pltpu.VMEM)
-    smem = pl.BlockSpec(memory_space=pltpu.SMEM)
     dma = pltpu.SemaphoreType.DMA
     width = QH * DH
     shapes = [
@@ -534,23 +607,21 @@
         pltpu.VMEM((NG + 1, 1, Q2), F32),
         pltpu.VMEM((8, Q2), F32),
         pltpu.VMEM((8, Q2), F32),
-        pltpu.VMEM((NG + 2, 1, Q2), F32),
+        pltpu.VMEM((NG + 3, 1, Q2), F32),
         pltpu.VMEM((NG, GR, 2 * DH), F32),
-        pltpu.VMEM((NG, 2 * OWN, 2 * DH), BF),
-        pltpu.VMEM((NG, 2 * OWN, 2 * DH), BF),
-        pltpu.VMEM((OWN, 2 * DH), BF),
-        pltpu.VMEM((OWN, 2 * DH), BF),
-        pltpu.VMEM((7, OWN, 2 * DH), BF),
-        pltpu.VMEM((7, OWN, 2 * DH), BF),
+        pltpu.VMEM((NG, 2, OWN, 2 * DH), BF),
+        pltpu.VMEM((NG, 2, OWN, 2 * DH), BF),
+        pltpu.VMEM((9, OWN, 2 * DH), BF),
+        pltpu.VMEM((9, OWN, 2 * DH), BF),
         pltpu.VMEM((3, 8, 8, DH), F32),
-        dma((9,)), dma((8,)), dma((8,)), dma((8,)), dma((8,)), dma((5,)), dma((5,)),
-        dma((5,)), dma((5,)), dma((8,)), dma((8,)), dma((3, 8)), dma((3, 8)),
+        dma((9,)), dma((24,)), dma((24,)), dma((6,)), dma((6,)), dma((5,)), dma((5,)),
+        dma((NG, 2, 2)), dma((NG, 2, 2)), dma((18,)), dma((18,)), dma((3, 8)), dma((3, 8)),
     ]
     anywhere = pl.BlockSpec(memory_space=pl.ANY)
     res = pl.pallas_call(
         kernel,
         out_shape=shapes,
-        in_specs=[anywhere] + [vmem] * 4 + [smem] + [vmem] * 2 + [anywhere],
+        in_specs=[anywhere] + [vmem] * 7 + [anywhere],
         out_specs=[anywhere] * 7,
         scratch_shapes=scratch,
         compiler_params=pltpu.CompilerParams(

time: 56.6 us -> 54.4 us (0.961)
  the two profiles are of different devices: /device:TPU:1 before, /device:TPU:2 now
where the time goes in v3:
time: 54.4 us; the launch traced here: 54.2 us
  Pallas kernels  52.9 us (97%)
  between operations  1.29 us (2%)
    pallas_call x1, Pallas kernels, per_device(): pl.pallas_call(kernel, out_shape=shapes, in_specs=[anywhere] + [vmem] * 7...  51.1 us
    pallas_call x1, Pallas kernels, per_device(): pl.pallas_call(place, out_shape=shapes, in_specs=[anywhere] * 7, out_spec...  1.89 us

profile of v3, /device:TPU:2, one launch (start us, length us, event | category | flops | bytes accessed | tf_op | source)
XLA Modules:
  0.0 54.2 jit_solution(12706663109128883527)
XLA Ops:
  1.3 51.1 %shard_map.144 = (bf16[128,1024]{1,0:T(8,128)(2,1)}, bf16[128,1024]{1,0:T(8,128)(2,1)}, bf16[128,128]{1,0:T(8,128)(2,1)}, bf16[128,128]{1,0:T(8,128)(2,1)}, bf16...) custom-call(bf16[128,1024]{1,0:T(8,128)(2,1)} %bitcast.14, bf16[128,128]{1,0:T(8,128)(2,1)} %bitcast.16, ...), custom_call_target="tpu_custom_call" | custom-call | tf_op jit(solution)/shard_map/pallas_call | solution.py:621
  52.3 1.9 %shard_map.145 = (bf16[128,1024]{1,0:T(8,128)(2,1)}, bf16[128,1024]{1,0:T(8,128)(2,1)}, bf16[128,128]{1,0:T(8,128)(2,1)}, bf16[128,128]{1,0:T(8,128)(2,1)}, bf16...) custom-call(bf16[128,1024]{1,0:T(8,128)(2,1)} %get-tuple-element.21.refs_0_, ...), custom_call_target="tpu_custom_call" | custom-call | tf_op jit(solution)/shard_map/pallas_call | solution.py:641

commit v4 on v3

--- a/solution.py
+++ b/solution.py
@@ -57,17 +57,24 @@
 
 
 def kernel(
-    cq_hbm, ck, cv, pk, pv, live_ref, q_gain, k_gain, dout_hbm,
+    cq_hbm, ck_hbm, cv_hbm, pk_hbm, pv_hbm, live_hbm, q_gain_hbm, k_gain_hbm, dout_hbm,
     out_hbm, dq_hbm, dck_hbm, dcv_hbm, dpk_hbm, dpv_hbm, gains_hbm,
-    cq, d_out, out, dq, dck, dcv, dpk, dpv, gains,
-    kv, q, do, ownkv, trans, s_buf, e_buf, f_buf, dp_buf, e_own, dp_own, ok_t, dq_t, o_rem, dq_rem, m_run,
+    cq, ck, cv, pk, pv, live_ref, q_gain, k_gain, d_out, out, dq, dck, dcv, dpk, dpv, gains,
+    kv, q, do, ownkv, trans, trans_half, trans_own, s_buf, e_buf, f_buf, dp_buf, e_own, dp_own, ok_t, dq_t, o_rem, dq_rem, m_run,
     m_at, stat, stat_rem, fac, part, y_out, y_in, z_out, z_in, g_buf,
     io_s, za_s, za_r, y_s, y_r, c_s, c_r, ry_s, ry_r, rz_s, rz_r, g_s, g_r,
 ):
-    read_q = pltpu.make_async_copy(cq_hbm, cq, io_s.at[0])
-    read_d = pltpu.make_async_copy(dout_hbm, d_out, io_s.at[1])
-    read_q.start()
-    read_d.start()
+    reads = [
+        pltpu.make_async_copy(src, dst, io_s.at[9 + i])
+        for i, (src, dst) in enumerate(
+            (
+                (pk_hbm, pk), (k_gain_hbm, k_gain), (pv_hbm, pv), (cq_hbm, cq), (q_gain_hbm, q_gain),
+                (live_hbm, live_ref), (dout_hbm, d_out), (ck_hbm, ck), (cv_hbm, cv),
+            )
+        )
+    ]
+    for r in reads:
+        r.start()
 
     sample = lax.axis_index("sample")
     px = lax.axis_index("prompt")
@@ -106,8 +113,9 @@
                 barrier, inc=1, device_id=partner(r, lax.rem(my_slot[r] + k, 8)), device_id_type=MESH
             )
 
+    for r in reads[0:3]:
+        r.wait()
     kg = k_gain[...]
-    qg = q_gain[...]
     pk_raw = pk[...].astype(F32)
     kv[0:OWN, 0:DH] = (pk_raw * rms(pk_raw) * kg).astype(BF)
     kv[0:OWN, DH:] = pv[...]
@@ -157,33 +165,37 @@
     copy_y(0).start()
     copy_y(1).start()
 
+    for r in reads[3:6]:
+        r.wait()
+    qg = q_gain[...]
     live_rows = lax.broadcasted_iota(jnp.int32, (TOK, 1), 0) < live_ref[...]
-    read_q.wait()
     for h in range(QH):
         x = cq[:, h * DH : (h + 1) * DH].astype(F32)
         q[h * TOK : (h + 1) * TOK, :] = (x * rms(x) * qg).astype(BF)
     copy_q = send(q.at[0:NQ, :], q.at[NQ:, :], c_s.at[0], c_r.at[0], sib)
     copy_q.start()
-    read_d.wait()
+    reads[6].wait()
     for h in range(QH):
         g = d_out[:, h * DH : (h + 1) * DH]
         do[h * TOK : (h + 1) * TOK, :] = jnp.where(live_rows, g, jnp.zeros_like(g))
     copy_do = send(do.at[0:NQ, :], do.at[NQ:, :], c_s.at[1], c_r.at[1], sib)
     copy_do.start()
 
+    reads[7].wait()
+    reads[8].wait()
     ck_raw = ck[...].astype(F32)
     ownkv[:, 0:DH] = (ck_raw * rms(ck_raw) * kg).astype(BF)
     ownkv[:, DH:] = cv[...]
 
-    def turn(keys, vals, count):
-        trans[0:DH, 0:count] = vals.astype(F32).T.astype(BF)
-        trans[DH:, 0:count] = keys.astype(F32).T.astype(BF)
+    def turn(keys, vals, into):
+        into[0:DH, :] = vals.astype(F32).T.astype(BF)
+        into[DH:, :] = keys.astype(F32).T.astype(BF)
 
     m_run[...] = jnp.full((1, Q2), LOW, F32)
     stat[...] = jnp.zeros((8, Q2), F32)
     ok_t[:, NQ:] = jnp.zeros((2 * DH, NQ), F32)
     dq_t[:, NQ:] = jnp.zeros((DH, NQ), F32)
-    turn(ownkv[:, 0:DH], ownkv[:, DH:], TOK)
+    turn(ownkv[:, 0:DH], ownkv[:, DH:], trans_own)
     u_ids = lax.broadcasted_iota(jnp.int32, (TOK, QB), 0)
     t_ids = lax.rem(lax.broadcasted_iota(jnp.int32, (TOK, QB), 1), TOK)
     allowed = u_ids <= t_ids
@@ -200,24 +212,14 @@
         m_run[:, sl] = m
         stat[1:2, sl] = jnp.sum(e, axis=0, keepdims=True)
         stat[2:3, sl] = jnp.sum(ed, axis=0, keepdims=True)
-        ok_t[:, sl] = dot(trans[:, 0:TOK], eb, NN)
-        dq_t[:, sl] = dot(trans[DH:, 0:TOK], ed.astype(BF), NN)
+        ok_t[:, sl] = dot(trans_own[...], eb, NN)
+        dq_t[:, sl] = dot(trans_own[DH:, :], ed.astype(BF), NN)
     m_at[NG] = m_run[...]
 
     for h in range(2):
         copy_y(h).wait_recv()
         copy_z(14 + h).start()
         copy_z(16 + h).start()
-    for h in range(2):
-        copy_z(4 + h).wait_recv()
-        copy_z(6 + h).wait_recv()
-        for i in (8 + h, 12 + h, 10 + h):
-            copy_z(i).start()
-    for h in range(2):
-        copy_z(h).wait_recv()
-        copy_z(2 + h).wait_recv()
-        copy_y(2 + h).start()
-        copy_y(4 + h).start()
     copy_q.wait_recv()
     copy_do.wait_recv()
 
@@ -234,23 +236,58 @@
 
     def scores(b, at_rows, keys, vals):
         s = dot(keys, q[tile(b), :], NT)
-        s_buf[:, tile(b)] = s
+        s_buf[0 : keys.shape[0], tile(b)] = s
         dp_buf[at_rows, tile(b)] = dot(vals, do[tile(b), :], NT)
         return jnp.max(s, axis=0, keepdims=True)
 
-    def weigh(b, at_rows, al, mc):
+    def weigh(b, at_rows, al, mc, count):
         sl = tile(b)
-        e = jnp.exp2(s_buf[:, sl] * C2 - mc)
+        e = jnp.exp2(s_buf[0:count, sl] * C2 - mc)
         ed = e * dp_buf[at_rows, sl]
         e_buf[at_rows, sl] = e.astype(BF)
-        f_buf[:, sl] = ed.astype(BF)
+        f_buf[0:count, sl] = ed.astype(BF)
         stat[1:2, sl] = stat[1:2, sl] * al + jnp.sum(e, axis=0, keepdims=True)
         stat[2:3, sl] = stat[2:3, sl] * al + jnp.sum(ed, axis=0, keepdims=True)
 
-    def mix(b, at_rows, al):
+    def mix(b, at_rows, al, turned, count):
         sl = tile(b)
-        ok_t[:, sl] = ok_t[:, sl] * al + dot(trans[...], e_buf[at_rows, sl], NN)
-        dq_t[:, sl] = dq_t[:, sl] * al + dot(trans[DH:, :], f_buf[:, sl], NN)
+        ok_t[:, sl] = ok_t[:, sl] * al + dot(turned[...], e_buf[at_rows, sl], NN)
+        dq_t[:, sl] = dq_t[:, sl] * al + dot(turned[DH:, :], f_buf[0:count, sl], NN)
+
+    def attend(at_rows, turned, count):
+        keys = kv[at_rows, 0:DH]
+        vals = kv[at_rows, DH:]
+        turn(keys, vals, turned)
+        mx, al, mc = {}, {}, {}
+        for t in range(tiles + 2):
+            if 1 <= t <= tiles:
+                al[t - 1], mc[t - 1] = rise(t - 1, mx[t - 1])
+            if t < tiles:
+                mx[t] = scores(t, at_rows, keys, vals)
+            if 1 <= t <= tiles:
+                weigh(t - 1, at_rows, al[t - 1], mc[t - 1], count)
+            if t >= 2:
+                mix(t - 2, at_rows, al[t - 2], turned, count)
+
+    def forward_half(i, carry):
+        @pl.when(i == 1)
+        def _():
+            for h in range(2):
+                copy_z(4 + h).wait_recv()
+                copy_z(6 + h).wait_recv()
+                for i in (8 + h, 12 + h, 10 + h):
+                    copy_z(i).start()
+            for h in range(2):
+                copy_z(h).wait_recv()
+                copy_z(2 + h).wait_recv()
+                copy_y(2 + h).start()
+                copy_y(4 + h).start()
+
+        attend(pl.ds(pl.multiple_of(i * (GR // 2), GR // 2), GR // 2), trans_half, GR // 2)
+        m_at[i * (NG + 1)] = m_run[...]
+        return carry
+
+    lax.fori_loop(0, 2, forward_half, 0)
 
     def forward(g, carry):
         @pl.when(g == 1)
@@ -268,24 +305,11 @@
             for i in range(8, 12):
                 copy_z(i).wait_recv()
 
-        at_rows = pl.ds(pl.multiple_of(g * GR, GR), GR)
-        keys = kv[at_rows, 0:DH]
-        vals = kv[at_rows, DH:]
-        turn(keys, vals, GR)
-        mx, al, mc = {}, {}, {}
-        for t in range(tiles + 2):
-            if 1 <= t <= tiles:
-                al[t - 1], mc[t - 1] = rise(t - 1, mx[t - 1])
-            if t < tiles:
-                mx[t] = scores(t, at_rows, keys, vals)
-            if 1 <= t <= tiles:
-                weigh(t - 1, at_rows, al[t - 1], mc[t - 1])
-            if t >= 2:
-                mix(t - 2, at_rows, al[t - 2])
+        attend(pl.ds(pl.multiple_of(g * GR, GR), GR), trans, GR)
         m_at[g] = m_run[...]
         return carry
 
-    lax.fori_loop(0, NG - 1, forward, 0)
+    lax.fori_loop(1, NG - 1, forward, 0)
 
     for i in (12, 13, 18, 19, 20, 21, 22, 23):
         copy_z(i).wait_recv()
@@ -299,15 +323,15 @@
         if t < tiles:
             mx[t] = scores(t, last, keys, vals)
         if t >= 1:
-            weigh(t - 1, last, al[t - 1], mc[t - 1])
+            weigh(t - 1, last, al[t - 1], mc[t - 1], GR)
     m_at[NG - 1] = m_run[...]
 
     stat[0:1, :] = m_run[...]
     copy_st = send(stat, stat_rem, c_s.at[2], c_r.at[2], sib)
     copy_st.start()
-    turn(keys, vals, GR)
+    turn(keys, vals, trans)
     for b in range(tiles):
-        mix(b, last, al[b])
+        mix(b, last, al[b], trans, GR)
     copy_st.wait_recv()
     for half in range(2):
         mine = slice(half * NQ, (half + 1) * NQ)
@@ -320,6 +344,7 @@
             fac[i, :, mine] = jnp.exp2((m_at[i, :, mine] - m_f) * C2) * inv
         fac[NG + 1, :, mine] = (stat[2:3, mine] * w_a + stat_rem[2:3, other] * w_b) * inv
         fac[NG + 2, :, mine] = w_a * inv
+        fac[NG + 3, :, mine] = jnp.exp2((m_at[NG + 1, :, mine] - m_f) * C2) * inv
 
     def g_start(r, value):
         g_buf[r, my_slot[r]] = value
@@ -371,11 +396,13 @@
         return send(z_out.at[at_slot], z_in.at[at_slot], rz_s.at[i], rz_r.at[i], z_dev(to))
 
     def gradients(g, at_rows):
+        low = g + (NG + 3) * (1 - jnp.minimum(g, 1))
         dk = jnp.zeros((GR, DH), F32)
         dv = jnp.zeros((GR, DH), F32)
         for b in range(tiles):
             sl = tile(b)
-            p = e_buf[at_rows, sl].astype(F32) * fac[g, :, sl]
+            e = e_buf[at_rows, sl].astype(F32)
+            p = jnp.concatenate([e[: GR // 2] * fac[g, :, sl], e[GR // 2 :] * fac[low, :, sl]], axis=0)
             pb = p.astype(BF)
             ds = (p * (dp_buf[at_rows, sl] - fac[NG + 1, :, sl])).astype(BF)
             dv = dv + dot(pb, do[sl, :], NN)
@@ -566,7 +593,6 @@
 
 
 def per_device(comp_q, comp_k, comp_v, prompt_k, prompt_v, lengths, q_gain, k_gain, d_out):
-    vmem = pl.BlockSpec(memory_space=pltpu.VMEM)
     dma = pltpu.SemaphoreType.DMA
     width = QH * DH
     shapes = [
@@ -580,6 +606,13 @@
     ]
     scratch = [
         pltpu.VMEM((TOK, width), BF),
+        pltpu.VMEM((TOK, DH), BF),
+        pltpu.VMEM((TOK, DH), BF),
+        pltpu.VMEM((OWN, DH), BF),
+        pltpu.VMEM((OWN, DH), BF),
+        pltpu.VMEM((1, 1), jnp.int32),
+        pltpu.VMEM((1, DH), F32),
+        pltpu.VMEM((1, DH), F32),
         pltpu.VMEM((TOK, width), BF),
         pltpu.VMEM((TOK, width), BF),
         pltpu.VMEM((TOK, width), BF),
@@ -593,6 +626,8 @@
         pltpu.VMEM((Q2, DH), BF),
         pltpu.VMEM((TOK, 2 * DH), BF),
         pltpu.VMEM((2 * DH, GR), BF),
+        pltpu.VMEM((2 * DH, GR // 2), BF),
+        pltpu.VMEM((2 * DH, TOK), BF),
         pltpu.VMEM((GR, Q2), F32),
         pltpu.VMEM((KEYS, Q2), BF),
         pltpu.VMEM((GR, Q2), BF),
@@ -604,24 +639,24 @@
         pltpu.VMEM((DH, NQ), F32),
         pltpu.VMEM((DH, NQ), F32),
         pltpu.VMEM((1, Q2), F32),
-        pltpu.VMEM((NG + 1, 1, Q2), F32),
+        pltpu.VMEM((NG + 2, 1, Q2), F32),
         pltpu.VMEM((8, Q2), F32),
         pltpu.VMEM((8, Q2), F32),
-        pltpu.VMEM((NG + 3, 1, Q2), F32),
+        pltpu.VMEM((NG + 4, 1, Q2), F32),
         pltpu.VMEM((NG, GR, 2 * DH), F32),
         pltpu.VMEM((NG, 2, OWN, 2 * DH), BF),
         pltpu.VMEM((NG, 2, OWN, 2 * DH), BF),
         pltpu.VMEM((9, OWN, 2 * DH), BF),
         pltpu.VMEM((9, OWN, 2 * DH), BF),
         pltpu.VMEM((3, 8, 8, DH), F32),
-        dma((9,)), dma((24,)), dma((24,)), dma((6,)), dma((6,)), dma((5,)), dma((5,)),
+        dma((18,)), dma((24,)), dma((24,)), dma((6,)), dma((6,)), dma((5,)), dma((5,)),
         dma((NG, 2, 2)), dma((NG, 2, 2)), dma((18,)), dma((18,)), dma((3, 8)), dma((3, 8)),
     ]
     anywhere = pl.BlockSpec(memory_space=pl.ANY)
     res = pl.pallas_call(
         kernel,
         out_shape=shapes,
-        in_specs=[anywhere] + [vmem] * 7 + [anywhere],
+        in_specs=[anywhere] * 9,
         out_specs=[anywhere] * 7,
         scratch_shapes=scratch,
         compiler_params=pltpu.CompilerParams(

time: 54.4 us -> 52.9 us (0.972)
  the two profiles are of different devices: /device:TPU:2 before, /device:TPU:4 now
where the time goes in v4:
time: 52.9 us; the launch traced here: 52.8 us
  Pallas kernels  51.5 us (97%)
  between operations  1.29 us (2%)
    pallas_call x1, Pallas kernels, per_device(): pl.pallas_call(kernel, out_shape=shapes, in_specs=[anywhere] * 9, out_spe...  49.6 us
    pallas_call x1, Pallas kernels, per_device(): pl.pallas_call(place, out_shape=shapes, in_specs=[anywhere] * 7, out_spec...  1.89 us

profile of v4, /device:TPU:4, one launch (start us, length us, event | category | flops | bytes accessed | tf_op | source)
XLA Modules:
  0.0 52.8 jit_solution(1019319935177967048)
XLA Ops:
  1.3 49.6 %shard_map.144 = (bf16[128,1024]{1,0:T(8,128)(2,1)}, bf16[128,1024]{1,0:T(8,128)(2,1)}, bf16[128,128]{1,0:T(8,128)(2,1)}, bf16[128,128]{1,0:T(8,128)(2,1)}, bf16...) custom-call(bf16[128,1024]{1,0:T(8,128)(2,1)} %bitcast.14, bf16[128,128]{1,0:T(8,128)(2,1)} %bitcast.16, ...), custom_call_target="tpu_custom_call" | custom-call | tf_op jit(solution)/shard_map/pallas_call | solution.py:656
  50.9 1.9 %shard_map.145 = (bf16[128,1024]{1,0:T(8,128)(2,1)}, bf16[128,1024]{1,0:T(8,128)(2,1)}, bf16[128,128]{1,0:T(8,128)(2,1)}, bf16[128,128]{1,0:T(8,128)(2,1)}, bf16...) custom-call(bf16[128,1024]{1,0:T(8,128)(2,1)} %get-tuple-element.21.refs_0_, ...), custom_call_target="tpu_custom_call" | custom-call | tf_op jit(solution)/shard_map/pallas_call | solution.py:676

commit v5 on v4

--- a/solution.py
+++ b/solution.py
@@ -27,6 +27,7 @@
 C2 = SCALE / math.log(2.0)
 LOW = -1e30
 MESH = pl.DeviceIdType.MESH
+FAR_FIRST = (4, 3, 5, 2, 6, 1, 7)
 
 
 def dot(a, b, dims):
@@ -107,8 +108,8 @@
         )
 
     barrier = pltpu.get_barrier_semaphore()
-    for r in (1, 2, 0):
-        for k in range(1, 8):
+    for k in FAR_FIRST:
+        for r in (1, 2, 0):
             pl.semaphore_signal(
                 barrier, inc=1, device_id=partner(r, lax.rem(my_slot[r] + k, 8)), device_id_type=MESH
             )
@@ -160,10 +161,10 @@
         dst, src = y_plan[i]
         return send(rows(src, HALF), rows(dst, HALF), y_s.at[i], y_r.at[i], ynb)
 
+    copy_y(0).start()
+    copy_y(1).start()
     for i in (4, 6, 5, 7, 0, 2, 1, 3):
         copy_z(i).start()
-    copy_y(0).start()
-    copy_y(1).start()
 
     for r in reads[3:6]:
         r.wait()
@@ -348,7 +349,7 @@
 
     def g_start(r, value):
         g_buf[r, my_slot[r]] = value
-        for k in range(1, 8):
+        for k in FAR_FIRST:
             send(
                 g_buf.at[r, my_slot[r]], g_buf.at[r, my_slot[r]], g_s.at[r, k], g_r.at[r, my_slot[r]],
                 partner(r, lax.rem(my_slot[r] + k, 8)),
@@ -415,9 +416,9 @@
     y_out[3, 1] = part[3, OWN : 2 * OWN, :].astype(BF)
     y_out[1, 0] = part[3, 3 * OWN :, :].astype(BF)
     for h in range(2):
+        copy_ry4(h).start()
         for c in copy_ry(3, h):
             c.start()
-        copy_ry4(h).start()
 
     own = fac[NG + 2]
     ok_t[0:DH, :] = ok_t[0:DH, :] * own
@@ -431,19 +432,18 @@
     g_start(0, jnp.sum(jnp.where(eye, pairs, 0.0).reshape(DH // 8, 8, DH), axis=0))
 
     def far_sums(h):
-        for c in copy_ry(3, h):
+        r = slice(h * HALF, (h + 1) * HALF)
+        copy_ry4(h).wait_recv()
+        start = 2 * OWN + h * HALF
+        z_out[6, r, :] = (part[3, start : start + HALF, :] + y_in[1, 0, r, :].astype(F32)).astype(BF)
+        copy_rz(12 + h).start()
+        for sign, c in enumerate(copy_ry(3, h)):
             c.wait_recv()
-        copy_ry4(h).wait_recv()
-        r = slice(h * HALF, (h + 1) * HALF)
-        for sign in range(2):
             start = (2 + sign) * OWN + h * HALF
             z_out[4 + sign, r, :] = (
                 part[2, start : start + HALF, :] + y_in[3, sign, r, :].astype(F32)
             ).astype(BF)
             copy_rz(8 + 2 * sign + h).start()
-        start = 2 * OWN + h * HALF
-        z_out[6, r, :] = (part[3, start : start + HALF, :] + y_in[1, 0, r, :].astype(F32)).astype(BF)
-        copy_rz(12 + h).start()
 
     def backward(i, carry):
         g = NG - 2 - i
@@ -469,12 +469,12 @@
 
     lax.fori_loop(0, NG - 1, backward, 0)
 
+    g_start(1, g_wait(0))
     far_sums(1)
     z_out[0] = part[0, 2 * OWN : 3 * OWN, :].astype(BF)
     z_out[1] = part[0, 3 * OWN :, :].astype(BF)
     for j in range(4):
         copy_rz(j).start()
-    g_start(1, g_wait(0))
 
     dk = jnp.zeros((TOK, DH), F32)
     dv = jnp.zeros((TOK, DH), F32)
@@ -502,7 +502,6 @@
     write_o = pltpu.make_async_copy(out, out_hbm, io_s.at[4])
     write_o.start()
 
-    g_start(2, g_wait(1))
     for j in range(14, 18):
         copy_rz(j).wait_recv()
     y_out[0, 0] = (
@@ -525,6 +524,7 @@
             z_out[2 + sign, r, :] = acc.astype(BF)
             copy_rz(4 + 2 * sign + h).start()
 
+    g_start(2, g_wait(1))
     copy_dq.wait_recv()
     for h in range(QH):
         sl = slice(h * TOK, (h + 1) * TOK)

time: 52.9 us -> 51 us (0.964)
  the two profiles are of different devices: /device:TPU:4 before, /device:TPU:1 now
where the time goes in v5:
time: 51 us; the launch traced here: 50.9 us
  Pallas kernels  49.6 us (97%)
  between operations  1.29 us (3%)
    pallas_call x1, Pallas kernels, per_device(): pl.pallas_call(kernel, out_shape=shapes, in_specs=[anywhere] * 9, out_spe...  47.7 us
    pallas_call x1, Pallas kernels, per_device(): pl.pallas_call(place, out_shape=shapes, in_specs=[anywhere] * 7, out_spec...  1.89 us

profile of v5, /device:TPU:1, one launch (start us, length us, event | category | flops | bytes accessed | tf_op | source)
XLA Modules:
  0.0 50.9 jit_solution(12029576915981347508)
XLA Ops:
  1.3 47.7 %shard_map.144 = (bf16[128,1024]{1,0:T(8,128)(2,1)}, bf16[128,1024]{1,0:T(8,128)(2,1)}, bf16[128,128]{1,0:T(8,128)(2,1)}, bf16[128,128]{1,0:T(8,128)(2,1)}, bf16...) custom-call(bf16[128,1024]{1,0:T(8,128)(2,1)} %bitcast.14, bf16[128,128]{1,0:T(8,128)(2,1)} %bitcast.16, ...), custom_call_target="tpu_custom_call" | custom-call | tf_op jit(solution)/shard_map/pallas_call | solution.py:656
  49.0 1.9 %shard_map.145 = (bf16[128,1024]{1,0:T(8,128)(2,1)}, bf16[128,1024]{1,0:T(8,128)(2,1)}, bf16[128,128]{1,0:T(8,128)(2,1)}, bf16[128,128]{1,0:T(8,128)(2,1)}, bf16...) custom-call(bf16[128,1024]{1,0:T(8,128)(2,1)} %get-tuple-element.21.refs_0_, ...), custom_call_target="tpu_custom_call" | custom-call | tf_op jit(solution)/shard_map/pallas_call | solution.py:676
